TPU v7x, 512 devices: a whole 4x4x16 slice. The times are simulated.
512 devices in a mesh: ctx: 128 (over x_lo, y, z), rep: 4 (over x_hi, core).
Axes of the slice: x: 4 (x_hi: 2, x_lo: 2; x = x_hi * 2 + x_lo), y: 4, z: 16, core: 2. Of those that a mesh axis runs over, the one named last changes fastest.
Arguments:
- projected: bfloat16 [3, 4096, 16384], P(None, 'rep', 'ctx'), may hold values from -6 to 6
- short_taps: float32 [3, 4096, 3], P(None, 'rep'), may hold values from -3 to 3
- residues: float32 [4096, 16], P('rep'), may hold values from -1.5 to 1.5
- decay_rates: float32 [4096, 16], P('rep'), may hold values from 0 to 1, as said below
- skip_gain: float32 [4096], P('rep'), may hold values from -4 to 4
- out_weight: bfloat16 [4096, 4096], P('ctx', 'rep'), may hold values from -0.09375 to 0.09375
Outputs:
- mixed_out: bfloat16 [4096, 16384], P('rep', 'ctx')
Inputs may be any that keep to these rules, and one draw needn't show every extreme that they name: `decay_rates`: positive decay rates, none above 1/30.
All inputs are finite; a program needn't handle non-finite values.
Results may differ from a plain program's by a relative error of at most 0.015.
Values may be sent and summed in bfloat16 or wider, within the bound.
A program may use at most 128 MiB of HBM per device.

v0:
```python
import math

import jax
import jax.numpy as jnp
from jax import lax
from jax.sharding import PartitionSpec as P

PRECISE = lax.Precision.HIGHEST


def shifted(x, axis, by):
    peers = lax.axis_size(axis)
    pairs = [(i, i + by) for i in range(peers) if 0 <= i + by < peers]
    return lax.ppermute(x, axis, pairs)


def angle_table(first_count, second_count, modulus):
    left_index = jnp.arange(first_count, dtype=jnp.int32)[:, None]
    right_index = jnp.arange(second_count, dtype=jnp.int32)[None, :]
    angle = (left_index * right_index % modulus).astype(jnp.float32) * (2.0 * math.pi / modulus)
    return (jnp.cos(angle), -jnp.sin(angle))


def featurize(raw_streams, taps, previous):
    tap_count = taps.shape[2]
    length = raw_streams.shape[2]
    widened = jnp.concatenate([previous, raw_streams], axis=2).astype(jnp.float32)
    running = taps[:, :, 0:1] * widened[:, :, tap_count - 1 :]
    for offset in range(1, tap_count):
        begin = tap_count - 1 - offset
        running = running + taps[:, :, offset : offset + 1] * widened[:, :, begin : begin + length]
    return running


def mode_sum(weights, rates, offsets):
    total = jnp.zeros((weights.shape[0], offsets.shape[0]), jnp.float32)
    for mode_index in range(weights.shape[1]):
        total = total + weights[:, mode_index][:, None] * jnp.exp(
            -rates[:, mode_index][:, None] * offsets[None, :]
        )
    return total


def right_times(stacked, table):
    return jnp.einsum("ckn,nj->ckj", stacked, table, precision=PRECISE)


def long_mix(product, residues_own, rates_own, skip_own, splits):
    chan_count, length = product.shape
    inner = 2 * length // splits
    half = splits // 2
    modulus = 2 * length
    cosine_rows, sine_rows = angle_table(splits, splits, splits)
    cosine_cols, sine_cols = angle_table(inner, inner, inner)
    twist_cosine, twist_sine = angle_table(splits, inner, modulus)

    def forward(signal):
        shaped = signal.reshape(chan_count, half, inner)
        step_real = jnp.einsum("kn,cnm->ckm", cosine_rows[:, :half], shaped, precision=PRECISE)
        step_imag = jnp.einsum("kn,cnm->ckm", sine_rows[:, :half], shaped, precision=PRECISE)
        turned_real = step_real * twist_cosine - step_imag * twist_sine
        turned_imag = step_real * twist_sine + step_imag * twist_cosine
        outer_real = right_times(turned_real, cosine_cols) - right_times(turned_imag, sine_cols)
        outer_imag = right_times(turned_real, sine_cols) + right_times(turned_imag, cosine_cols)
        return (outer_real, outer_imag)

    signal = product.astype(jnp.float32)
    positions = jnp.arange(length).astype(jnp.float32)
    weighting = residues_own * jnp.sqrt(2.0 * rates_own)
    impulse = mode_sum(weighting, rates_own, positions)
    signal_real, signal_imag = forward(signal)
    impulse_real, impulse_imag = forward(impulse)
    joint_real = signal_real * impulse_real - signal_imag * impulse_imag
    joint_imag = signal_real * impulse_imag + signal_imag * impulse_real
    inner_real = right_times(joint_real, cosine_cols) + right_times(joint_imag, sine_cols)
    inner_imag = right_times(joint_imag, cosine_cols) - right_times(joint_real, sine_cols)
    back_real = inner_real * twist_cosine + inner_imag * twist_sine
    back_imag = inner_imag * twist_cosine - inner_real * twist_sine
    result = jnp.einsum("nk,ckm->cnm", cosine_rows[:half], back_real, precision=PRECISE)
    result = result + jnp.einsum("nk,ckm->cnm", sine_rows[:half], back_imag, precision=PRECISE)
    convolved = result.reshape(chan_count, length) / modulus
    return (convolved + skip_own[:, None] * signal).astype(jnp.bfloat16)


def per_device(projected, short_taps, residues, decay_rates, skip_gain, out_weight):
    channels = projected.shape[1]
    tok_count = projected.shape[2]
    splits = lax.axis_size("ctx")
    owned_count = channels // splits
    position = lax.axis_index("ctx")
    anchor = position * owned_count
    residues_own = lax.dynamic_slice_in_dim(residues, anchor, owned_count, 0)
    rates_own = lax.dynamic_slice_in_dim(decay_rates, anchor, owned_count, 0)
    skip_own = lax.dynamic_slice_in_dim(skip_gain, anchor, owned_count, 0)
    rim_width = short_taps.shape[2] - 1
    previous = shifted(projected[:, :, tok_count - rim_width :], "ctx", 1)
    featured = featurize(projected, short_taps, previous)
    gate_stream = featured[0].astype(jnp.bfloat16)
    product = (featured[1] * featured[2]).astype(jnp.bfloat16)
    arrived = lax.all_to_all(
        jnp.stack([gate_stream, product]), "ctx", split_axis=1, concat_axis=2, tiled=True
    )
    mixed_long = long_mix(arrived[1], residues_own, rates_own, skip_own, splits)
    gated = (arrived[0].astype(jnp.float32) * mixed_long.astype(jnp.float32)).astype(jnp.bfloat16)
    gated_home = lax.all_to_all(gated, "ctx", split_axis=1, concat_axis=0, tiled=True)
    gated_all = lax.all_gather(gated_home, "rep", axis=0, tiled=True)
    summed = lax.dot_general(
        lax.all_gather(out_weight, "ctx", axis=0, tiled=True),
        gated_all,
        (((0,), (0,)), ((), ())),
        preferred_element_type=jnp.float32,
    )
    return summed.astype(jnp.bfloat16)


def solution(mesh):
    in_specs = (
        P(None, "rep", "ctx"),
        P(None, "rep", None),
        P("rep", None),
        P("rep", None),
        P("rep"),
        P("ctx", "rep"),
    )
    out_specs = P("rep", "ctx")
    return jax.shard_map(
        per_device, mesh=mesh, in_specs=in_specs, out_specs=out_specs, check_vma=False
    )
```

profile of v0, /device:TPU:4, one launch (start us, length us, event | category | flops | bytes accessed | tf_op | source)
XLA Modules:
  0.0 772.7 jit_solution(17807919426622769703)
XLA Ops:
  6.5 1.5 slice.154
  8.4 3.8 collective-permute-start
  13.1 0.8 sqrt_multiply_fusion
  16.0 1.1 copy.167
  17.9 1.8 maximum_convert_fusion
  19.6 6.0 fusion
  25.6 0.8 fusion.12
  27.0 2.0 pad_maximum_fusion
  29.0 19.7 %all-to-all-start = ((bf16[2,1024,128]{2,0,1:T(2,128)(2,1)}), bf16[2,1024,128]{2,0,1:T(2,128)(2,1)S(1)}, u32[]{:S(2)}, u32[]{:S(2)}) async-start(bf16[2,1024,128]{2,0,1:T(2,128)(2,1)} %pad_maximum_fusion), calls=%async_computation | async-start | bytes 1048576 | tf_op jit(solution)/shard_map/all_to_all | solution.py:100
  48.9 1.4 fusion.78
  51.7 3.1 convolution_bitcast_fusion.1
  54.8 3.1 convolution_bitcast_fusion
  57.9 2.7 fusion.37
  60.7 3.0 fusion.25
  63.6 2.7 convolution_subtract_fusion.1
  66.4 2.7 convolution_add_fusion.1
  69.1 11.7 %all-to-all-done = bf16[2,1024,128]{2,0,1:T(2,128)(2,1)S(1)} async-done(((bf16[2,1024,128]{2,0,1:T(2,128)(2,1)}), bf16[2,1024,128]{2,0,1:T(2,128)(2,1)S(1)}, u32[]{:S(2)}, u32[]{:S(2)}) %all-to-all-start) | async-done | bytes 524320 | tf_op jit(solution)/shard_map/all_to_all | solution.py:100
  82.4 2.8 fusion.39
  85.2 3.2 fusion.27
  88.4 2.8 convolution_subtract_fusion.2
  91.2 3.0 multiply_subtract_fusion
  94.1 2.1 fusion.33
  96.2 2.1 fusion.31
  98.3 2.2 convolution_add_fusion
  100.5 2.1 convolution_subtract_fusion
  102.6 1.4 fusion.8
  104.0 1.4 fusion.3
  105.8 29.6 %all_to_all.31 = bf16[8,128,128]{2,0,1:T(8,128)(2,1)} all-to-all(bf16[8,128,128]{2,0,1:T(8,128)(2,1)S(1)} %fusion.15), channel_id=1, replica_groups=mesh['ctx'=128,'rep'=4] {'ctx'}, dimensions={1} | all-to-all | bytes 524288 | tf_op jit(solution)/shard_map/all_to_all | solution.py:105
  136.2 17.0 %all-gather.3.cloned.1.call-done = bf16[4096,128]{1,0:T(8,128)(2,1)} async-done(((bf16[1024,128]{1,0:T(8,128)(2,1)}), bf16[4096,128]{1,0:T(8,128)(2,1)}) %all-gather.3.cloned.1.call-update) | async-done | bytes 1048592 | tf_op jit(solution)/shard_map/all_gather | solution.py:106
  153.1 606.7 %all-gather.5.cloned.1.call-done = bf16[4096,1024]{1,0:T(8,128)(2,1)} async-done(((bf16[32,1024]{1,0:T(8,128)(2,1)}), bf16[4096,1024]{1,0:T(8,128)(2,1)}) %all-gather.5.cloned.1.call-update) | async-done | bytes 8388624 | tf_op jit(solution)/shard_map/all_gather | solution.py:108
  759.8 5.0 fusion.4
  764.8 0.8 copy.148
  (60 shorter events, 8.7 us)
Async XLA Ops:
  6.5 8.3 %copy-start = (bf16[3,1024,128]{2,1,0:T(8,128)(2,1)S(1)}, bf16[3,1024,128]{2,1,0:T(8,128)(2,1)}, u32[]{:S(2)}) copy-start(bf16[3,1024,128]{2,1,0:T(8,128)(2,1)} %param.6) | copy-start | bytes 2359300
  6.5 8.0 %copy-start.3 = (f32[3,1024,3]{1,2,0:T(4,128)S(1)}, f32[3,1024,3]{1,2,0:T(4,128)}, u32[]{:S(2)}) copy-start(f32[3,1024,3]{1,2,0:T(4,128)} %param.7) | copy-start | bytes 110596
  8.4 8.7 %collective-permute-start = (bf16[3,1024,2]{1,0,2:T(4,128)(2,1)S(1)}, bf16[3,1024,2]{1,0,2:T(4,128)(2,1)S(1)}, u32[]{:S(2)}, u32[]{:S(2)}) collective-permute-start(bf16[3,1024,2]{1,0,2:T(4,128)(2,1)S(1)} %copy.170), channel_id=1, source_target_pairs={{0,4},{4,8},{8,12},{12,16},{16,20},{20,24},{24,28},{28,32},{32,36}... | collective-permute-start | bytes 36872 | tf_op jit(solution)/shard_map/ppermute | solution.py:14
  17.8 1.8 copy-start.1
  26.5 25.1 %copy-start.2 = (f32[64,256]{1,0:T(8,128)S(1)}, f32[64,256]{1,0:T(8,128)}, u32[]{:S(2)}) copy-start(f32[64,256]{1,0:T(8,128)} %add_convert_fusion) | copy-start | bytes 196612
  26.5 25.1 %copy-start.4 = (f32[8]{0:T(128)S(1)}, f32[8]{0:T(128)}, u32[]{:S(2)}) copy-start(f32[8]{0:T(128)} %get-tuple-element.29) | copy-start | bytes 100
  26.5 25.1 %copy-start.5 = (f32[8]{0:T(128)S(1)}, f32[8]{0:T(128)}, u32[]{:S(2)}) copy-start(f32[8]{0:T(128)} %get-tuple-element.30) | copy-start | bytes 100
  26.5 25.1 %copy-start.6 = (f32[8]{0:T(128)S(1)}, f32[8]{0:T(128)}, u32[]{:S(2)}) copy-start(f32[8]{0:T(128)} %get-tuple-element.31) | copy-start | bytes 100
  26.5 25.1 %copy-start.7 = (f32[8]{0:T(128)S(1)}, f32[8]{0:T(128)}, u32[]{:S(2)}) copy-start(f32[8]{0:T(128)} %get-tuple-element.32) | copy-start | bytes 100
  26.5 25.1 %copy-start.8 = (f32[8]{0:T(128)S(1)}, f32[8]{0:T(128)}, u32[]{:S(2)}) copy-start(f32[8]{0:T(128)} %get-tuple-element.33) | copy-start | bytes 100
  26.5 25.1 %copy-start.9 = (f32[8]{0:T(128)S(1)}, f32[8]{0:T(128)}, u32[]{:S(2)}) copy-start(f32[8]{0:T(128)} %get-tuple-element.34) | copy-start | bytes 100
  26.5 25.1 %copy-start.10 = (f32[8]{0:T(128)S(1)}, f32[8]{0:T(128)}, u32[]{:S(2)}) copy-start(f32[8]{0:T(128)} %get-tuple-element.35) | copy-start | bytes 100
  26.5 25.1 %copy-start.11 = (f32[8]{0:T(128)S(1)}, f32[8]{0:T(128)}, u32[]{:S(2)}) copy-start(f32[8]{0:T(128)} %get-tuple-element.36) | copy-start | bytes 100
  26.6 25.1 %copy-start.12 = (f32[8]{0:T(128)S(1)}, f32[8]{0:T(128)}, u32[]{:S(2)}) copy-start(f32[8]{0:T(128)} %get-tuple-element.37) | copy-start | bytes 100
  26.6 25.1 %copy-start.13 = (f32[8]{0:T(128)S(1)}, f32[8]{0:T(128)}, u32[]{:S(2)}) copy-start(f32[8]{0:T(128)} %get-tuple-element.38) | copy-start | bytes 100
  26.6 25.1 %copy-start.14 = (f32[8]{0:T(128)S(1)}, f32[8]{0:T(128)}, u32[]{:S(2)}) copy-start(f32[8]{0:T(128)} %get-tuple-element.39) | copy-start | bytes 100
  26.6 25.1 %copy-start.15 = (f32[8]{0:T(128)S(1)}, f32[8]{0:T(128)}, u32[]{:S(2)}) copy-start(f32[8]{0:T(128)} %get-tuple-element.40) | copy-start | bytes 100
  26.6 25.1 %copy-start.16 = (f32[8]{0:T(128)S(1)}, f32[8]{0:T(128)}, u32[]{:S(2)}) copy-start(f32[8]{0:T(128)} %get-tuple-element.41) | copy-start | bytes 100
  29.0 51.8 %all-to-all-start = ((bf16[2,1024,128]{2,0,1:T(2,128)(2,1)}), bf16[2,1024,128]{2,0,1:T(2,128)(2,1)S(1)}, u32[]{:S(2)}, u32[]{:S(2)}) async-start(bf16[2,1024,128]{2,0,1:T(2,128)(2,1)} %pad_maximum_fusion), calls=%async_computation | async-start | bytes 1048576 | tf_op jit(solution)/shard_map/all_to_all | solution.py:100
  48.7 104.4 %all-gather.3.cloned.1.call-start = ((), (), s32[]{:S(2)}) async-start(), calls=%async_computation.2 | async-start | bytes 1310720 | tf_op jit(solution)/shard_map/all_gather | solution.py:106
  135.4 624.4 %all-gather.5.cloned.1.call-start = ((), (), s32[]{:S(2)}) async-start(), calls=%async_computation.3 | async-start | bytes 8454144 | tf_op jit(solution)/shard_map/all_gather | solution.py:108
Sparse Core Ops, SparseCore 0:
  135.5 17.5 all-gather.2
  155.2 604.5 all-gather.4
where the time goes:
time: 780 us; the launch traced here: 773 us
  waiting for transfers between devices  636 us (82%)
  matrix products  46.6 us (6%)
  blocking collectives  29.6 us (4%)
  starting transfers between devices  23.8 us (3%)
  other arithmetic  14.8 us (2%)
  between operations  14.1 us (2%)
    all_gather x1, waiting for transfers between devices, per_device(): lax.all_gather(out_weight, 'ctx', axis=0, tiled=True)  607 us
    dot_general x12, matrix products, right_times(): return jnp.einsum('ckn,nj->ckj', stacked, table, precision=PRECISE)  31.3 us
    all_to_all x1, blocking collectives, per_device(): lax.all_to_all(gated, 'ctx', split_axis=1, concat_axis=0, tiled=True)  29.6 us
    all_to_all x1, starting transfers between devices, per_device(): lax.all_to_all(jnp.stack([gate_stream, product]), 'ctx', split_axis=1, co...  19.7 us
    all_gather x1, waiting for transfers between devices, per_device(): gated_all = lax.all_gather(gated_home, 'rep', axis=0, tiled=True)  17 us
  transfers between devices with their start and end apart: 4, of which 3 were waited for; matrix products, arithmetic and copies ran while one was open for 3% of the time, Pallas kernels for 0%

commit v1 on v0

v1 whole, which is shorter than its diff:
```python
import math

import numpy as np
import jax
import jax.numpy as jnp
from jax import lax
from jax.experimental import pallas as pl
from jax.experimental.pallas import tpu as pltpu
from jax.sharding import PartitionSpec as P

X, Y, Z = 2, 4, 16
REPS = 4
MODES = 16
KC = 256
F32 = jnp.float32
BF16 = jnp.bfloat16
EXACT = lax.Precision.HIGHEST


def tables(length):
    k = np.arange(length)[:, None]
    t = np.arange(length)[None, :]
    angle = math.pi * ((2 * k + 1) * t % (4 * length)) / (2 * length)
    forward = np.concatenate([np.cos(angle), -np.sin(angle)], axis=0)
    return forward.astype(np.float32), (forward.T / length).astype(np.float32)


def kernel(
    proj, par, rates3, amps3, rate_tiles, fwd, bwd, w_shard, out,
    xs, halo_s, halo_r, prod, gate, spec, local, s_send, s_recv, t_send, t_recv, p_send, p_recv,
    gall, wg, acc, o_send, o_recv,
    halo_sem, s_ssem, s_rsem, t_ssem, t_rsem, p_ssem, p_rsem,
    w_rsem, wx_ssem, wy_ssem, wz_ssem, g_rsem, g_ssem, f_ssem, h_ssem, o_sem,
):
    chans, length = proj.shape[1], proj.shape[2]
    groups = chans // 128
    rows = w_shard.shape[0]
    half = w_shard.shape[1] // 2
    pieces = chans // KC
    steps = length // 8

    ctx = lax.axis_index("ctx")
    rep = lax.axis_index("rep")
    z = lax.rem(ctx, Z)
    y = lax.rem(ctx // Z, Y)
    xl = ctx // (Y * Z)
    xo = 1 - xl
    line = ctx // Z
    rep_core = rep + 1 - 2 * lax.rem(rep, 2)
    rep_far = rep + 2 - 4 * (rep // 2)

    def at(x_, y_, z_):
        return (x_ * Y + y_) * Z + z_

    def remote(src, dst, ssem, rsem, c, r=None):
        return pltpu.make_async_remote_copy(
            src_ref=src, dst_ref=dst, send_sem=ssem, recv_sem=rsem,
            device_id=(c, rep if r is None else r), device_id_type=pl.DeviceIdType.MESH,
        )

    nxt = lax.rem(ctx + 1, X * Y * Z)
    prv = lax.rem(ctx + X * Y * Z - 1, X * Y * Z)
    zr = at(xl, y, lax.rem(z + 1, Z))
    zl = at(xl, y, lax.rem(z + Z - 1, Z))

    bar = pltpu.get_barrier_semaphore()

    def hello(c, r):
        pl.semaphore_signal(bar, inc=1, device_id=(c, r), device_id_type=pl.DeviceIdType.MESH)

    hello(nxt, rep)
    hello(prv, rep)

    @pl.loop(1, Z)
    def _(d):
        hello(at(xl, y, lax.rem(z + d, Z)), rep)

    @pl.loop(1, X * Y)
    def _(d):
        hello(lax.rem(line + d, X * Y) * Z + z, rep)

    cx = at(xo, y, z)
    hello(ctx, rep_core)
    hello(cx, rep_far)
    pl.semaphore_wait(bar, 2 + (Z - 1) + (X * Y - 1) + 2)

    def wrow(b):
        return wg.at[pl.ds(pl.multiple_of(b * rows, rows), rows), :]

    def wblock(b, ssem, c):
        return remote(wrow(b), wrow(b), ssem, w_rsem.at[b], c)

    def wcols(i):
        return w_shard.at[:, pl.ds(pl.multiple_of(i * half, half), half)]

    other = ctx + (1 - 2 * xl) * (Y * Z)
    x_copy = remote(wcols(xo), wrow(ctx), wx_ssem.at[0], w_rsem.at[ctx], cx)
    x_copy.start()
    own = pltpu.make_async_copy(wcols(xl), wrow(ctx), wx_ssem.at[1])
    own.start()

    def a_blk(d_y, d_z):
        return at(0, lax.rem(y + d_y, Y), lax.rem(z + d_z + Z, Z))

    def b_blk(d_y, d_z):
        return at(1, lax.rem(y + d_y, Y), lax.rem(z + d_z + Z, Z))

    def peer_y(d):
        return at(xl, lax.rem(y + d, Y), z)

    def w_arrived(b):
        wblock(b, wx_ssem.at[0], ctx).wait_recv()

    def a_spread(d_z):
        b = a_blk(0, d_z)
        for j in range(1, Y):
            wblock(b, wy_ssem.at[(j - 1) * Z + lax.rem(d_z + Z, Z)], peer_y(j)).start()

    RZ = Z // 2

    def zs(part, right, k):
        return wz_ssem.at[(part * 2 + right) * RZ + k]

    def a_start():
        wblock(a_blk(0, 0), zs(0, 1, 0), zr).start()
        wblock(a_blk(0, 0), zs(0, 0, 0), zl).start()
        a_spread(0)

    def a_step(k):
        w_arrived(a_blk(0, -k))
        wblock(a_blk(0, -k), zs(0, 1, k), zr).start()
        a_spread(-k)
        w_arrived(a_blk(0, k))

        @pl.when(k < RZ - 1)
        def _():
            wblock(a_blk(0, k), zs(0, 0, k), zl).start()

        a_spread(k)

    def a_last():
        w_arrived(a_blk(0, -RZ))
        a_spread(-RZ)

    def b_begin():
        for j in range(1, Y):
            wblock(b_blk(0, 0), wy_ssem.at[(Y - 1) * Z + j - 1], peer_y(j)).start()

    def b_start():
        for j in range(Y):
            if j:
                w_arrived(b_blk(j, 0))
            wblock(b_blk(j, 0), zs(1 + j, 1, 0), zr).start()
            wblock(b_blk(j, 0), zs(1 + j, 0, 0), zl).start()

    def b_step(k):
        for j in range(Y):
            w_arrived(b_blk(j, -k))
            w_arrived(b_blk(j, k))
            right = (lambda j=j: wblock(b_blk(j, -k), zs(1 + j, 1, k), zr).start())
            left = (lambda j=j: wblock(b_blk(j, k), zs(1 + j, 0, k), zl).start())
            if j < Y // 2:
                right()
                pl.when(k < RZ - 1)(left)
            else:
                pl.when(k < RZ - 1)(right)
                left()

    def b_last():
        for j in range(Y):
            w_arrived(b_blk(j, RZ))

    def w_step(k):
        if k < RZ:
            a_step(k)
            b_step(k)

    eye = (
        lax.broadcasted_iota(jnp.int32, (length, length), 0)
        == lax.broadcasted_iota(jnp.int32, (length, length), 1)
    ).astype(BF16)

    def lanes(g, width=128):
        return pl.ds(pl.multiple_of(g * width, width), width)

    @pl.loop(0, groups)
    def _(g):
        for s in range(3):
            xs[s, pl.ds(8, length), lanes(g)] = lax.dot_general(
                eye, proj[s, lanes(g), :], (((1,), (1,)), ((), ())), preferred_element_type=F32
            )

    halo_s[...] = jnp.zeros_like(halo_s)
    for s in range(3):
        halo_s[pl.ds(2 * s, 2), :] = xs[s, pl.ds(8 + length - 2, 2), :]
    halo = remote(halo_s, halo_r, halo_sem.at[0], halo_sem.at[1], nxt)
    halo.start()

    own.wait()
    w_arrived(other)
    a_start()
    b_begin()

    sub = lax.broadcasted_iota(jnp.int32, (MODES, 8, 128), 1).astype(F32)

    @pl.loop(0, groups)
    def _(g):
        r = rates3[:, :, lanes(g)]
        w = amps3[:, :, lanes(g)] * jnp.sqrt(2.0 * r)
        q = w * jnp.exp(-r * sub)
        ratio = jnp.exp(-8.0 * r)
        for a in range(steps):
            local[pl.ds(8 * a, 8), lanes(g)] = jnp.sum(q, axis=0)
            q = q * ratio

    @pl.loop(0, groups)
    def _(g):
        spec[:, lanes(g)] = jnp.dot(
            fwd[...], local[:, lanes(g)], precision=EXACT, preferred_element_type=F32
        )

    b_start()

    halo.wait_recv()
    keep = jnp.where(ctx > 0, 1.0, 0.0).astype(F32)
    for s in range(3):
        xs[s, pl.ds(6, 2), :] = halo_r[pl.ds(2 * s, 2), :] * keep

    @pl.loop(0, groups)
    def _(g):
        made = []
        for s in range(3):
            total = par[pl.ds(3 * s, 1), lanes(g)] * xs[s, pl.ds(8, length), lanes(g)]
            for j in range(1, 3):
                total = total + (
                    par[pl.ds(3 * s + j, 1), lanes(g)] * xs[s, pl.ds(8 - j, length), lanes(g)]
                )
            made.append(total)
        gate[:, lanes(g)] = made[0].astype(BF16).astype(F32)
        prod[:, lanes(g)] = (made[1] * made[2]).astype(BF16).astype(F32)
        r = rates3[:, :, lanes(g)]
        ratio = jnp.exp(-8.0 * r)
        state = jnp.zeros((MODES, 8, 128), F32)
        for a in range(steps):
            state = state * ratio + prod[pl.ds(8 * a, 8), lanes(g)][None]
        ends = jnp.sum(state * jnp.exp(-r * (7.0 - sub)), axis=1)
        s_send[g] = ends[0:8]
        s_send[groups + g] = ends[8:16]

    s_recv[z] = s_send[z]

    @pl.loop(1, Z)
    def _(d):
        to = lax.rem(z + d, Z)
        remote(s_send.at[to], s_recv.at[z], s_ssem.at[d], s_rsem.at[z], at(xl, y, to)).start()

    w_step(1)

    @pl.loop(0, groups)
    def _(g):
        u = prod[:, lanes(g)]
        u_spec = jnp.dot(fwd[...], u, precision=EXACT, preferred_element_type=F32)
        h_spec = spec[:, lanes(g)]
        u_re, u_im = u_spec[:length], u_spec[length:]
        h_re, h_im = h_spec[:length], h_spec[length:]
        joint = jnp.concatenate(
            [u_re * h_re - u_im * h_im, u_re * h_im + u_im * h_re], axis=0
        )
        mixed = jnp.dot(bwd[...], joint, precision=EXACT, preferred_element_type=F32)
        local[:, lanes(g)] = mixed + par[pl.ds(9, 1), lanes(g)] * u

    @pl.loop(1, Z)
    def _(d):
        src = lax.rem(z + d, Z)
        remote(s_send.at[z], s_recv.at[src], s_ssem.at[d], s_rsem.at[src], ctx).wait_recv()

    tile_rate = rate_tiles[z]
    block_decay = jnp.exp(-float(length) * tile_rate)
    total = jnp.zeros((8, 128), F32)
    for i in range(Z):
        total = total * block_decay + s_recv[i]
    t_send[...] = total
    t_recv[line] = total

    @pl.loop(1, X * Y)
    def _(d):
        to = lax.rem(line + d, X * Y) * Z + z
        remote(t_send, t_recv.at[line], t_ssem.at[d], t_rsem.at[line], to).start()

    w_step(2)

    @pl.loop(1, X * Y)
    def _(d):
        src = lax.rem(line + d, X * Y)
        remote(t_send, t_recv.at[src], t_ssem.at[d], t_rsem.at[src], ctx).wait_recv()

    line_decay = jnp.exp(-float(length * Z) * tile_rate)
    carry = jnp.zeros((8, 128), F32)
    for i in range(X * Y):
        carry = jnp.where(i < line, carry * line_decay + t_recv[i], carry)
    for i in range(Z):
        p_send[i] = carry
        carry = carry * block_decay + s_recv[i]
    p_recv[z] = p_send[z]

    @pl.loop(1, Z)
    def _(d):
        to = lax.rem(z + d, Z)
        remote(p_send.at[to], p_recv.at[z], p_ssem.at[d], p_rsem.at[z], at(xl, y, to)).start()

    w_step(3)

    @pl.loop(1, Z)
    def _(d):
        src = lax.rem(z + d, Z)
        remote(p_send.at[z], p_recv.at[src], p_ssem.at[d], p_rsem.at[src], ctx).wait_recv()

    def piece(x_, r_, k):
        return gall.at[x_, r_, k]

    def g_copy(x_, r_, k, ssem, c, r):
        return remote(
            piece(x_, r_, k), piece(x_, r_, k), ssem, g_rsem.at[(x_ * REPS + r_) * pieces + k], c, r
        )

    def g_arrived(x_, r_, k):
        g_copy(x_, r_, k, g_ssem.at[0], ctx, rep).wait_recv()

    per = KC // 128

    def finish(k):
        for i in range(per):
            g = k * per + i
            r = rates3[:, :, lanes(g)]
            w = amps3[:, :, lanes(g)] * jnp.sqrt(2.0 * r)
            before = jnp.concatenate([p_recv[g], p_recv[groups + g]], axis=0)
            q = (w * jnp.exp(-r * (sub + 1.0))) * before[:, None, :]
            ratio = jnp.exp(-8.0 * r)
            for a in range(steps):
                here = (pl.ds(8 * a, 8), lanes(g))
                local[here] = local[here] + jnp.sum(q, axis=0)
                q = q * ratio
            long = local[:, lanes(g)].astype(BF16).astype(F32)
            gall[xl, rep, k, :, pl.ds(128 * i, 128)] = (gate[:, lanes(g)] * long).astype(BF16)

    @pl.loop(0, pieces)
    def _(k):
        finish(k)
        g_copy(xl, rep, k, g_ssem.at[3 * k], ctx, rep_core).start()
        g_copy(xl, rep, k, g_ssem.at[3 * k + 1], cx, rep).start()
        g_copy(xl, rep, k, g_ssem.at[3 * k + 2], cx, rep_far).start()

    @pl.loop(4, RZ)
    def _(k):
        a_step(k)
        b_step(k)

    a_last()
    b_last()

    @pl.loop(0, pieces)
    def _(k):
        g_arrived(xo, rep, k)

        @pl.when(lax.rem(k, 2) == 0)
        def _():
            g_copy(xo, rep, k, h_ssem.at[k], cx, rep_far).start()

        g_copy(xo, rep, k, f_ssem.at[3 * k], ctx, rep_core).start()
        g_arrived(xo, rep_far, k)

        @pl.when(lax.rem(k, 2) == 1)
        def _():
            g_copy(xo, rep_far, k, h_ssem.at[k], cx, rep).start()

        g_copy(xo, rep_far, k, f_ssem.at[3 * k + 1], ctx, rep_core).start()

    @pl.loop(0, pieces)
    def _(k):
        g_arrived(xl, rep_far, k)
        g_copy(xl, rep_far, k, f_ssem.at[3 * k + 2], ctx, rep_core).start()

    @pl.loop(0, Z)
    def _(d):
        for j in range(1, Y):
            w_arrived(a_blk(j, d))

    acc[...] = jnp.zeros_like(acc)

    def project(r_, k):
        c0 = (r_ * pieces + k) * KC
        w_part = wg[pl.ds(pl.multiple_of(c0, KC), KC), :]
        for x_ in range(X):
            acc[pl.ds(x_ * length, length), :] += jnp.dot(
                gall[x_, r_, k], w_part, preferred_element_type=F32
            )

    @pl.loop(0, pieces)
    def _(k):
        project(rep, k)

    @pl.loop(0, pieces)
    def _(k):
        project(rep_far, k)

    for src_rep in (rep_core, rep_far + rep_core - rep):
        @pl.loop(0, pieces)
        def _(k):
            g_arrived(xl, src_rep, k)
            g_arrived(xo, src_rep, k)
            project(src_rep, k)

    o_send[...] = acc[pl.ds(pl.multiple_of(xo * length, length), length), :].astype(BF16)
    swap = remote(o_send, o_recv, o_sem.at[0], o_sem.at[1], cx)
    swap.start()
    out[xl] = acc[pl.ds(pl.multiple_of(xl * length, length), length), :].astype(BF16)

    halo.wait_send()
    x_copy.wait_send()

    @pl.loop(1, Z)
    def _(d):
        remote(s_send.at[0], s_recv.at[0], s_ssem.at[d], s_rsem.at[0], ctx).wait_send()
        remote(p_send.at[0], p_recv.at[0], p_ssem.at[d], p_rsem.at[0], ctx).wait_send()

    @pl.loop(1, X * Y)
    def _(d):
        remote(t_send, t_recv.at[0], t_ssem.at[d], t_rsem.at[0], ctx).wait_send()

    @pl.loop(0, (Y - 1) * (Z + 1))
    def _(i):
        wblock(0, wy_ssem.at[i], ctx).wait_send()

    for part in range(1 + Y):
        for right in range(2):
            full = right == (1 if part <= Y // 2 else 0)

            @pl.loop(0, RZ if full else RZ - 1)
            def _(k):
                wblock(0, zs(part, right, k), ctx).wait_send()

    @pl.loop(0, 3 * pieces)
    def _(i):
        g_copy(0, 0, 0, g_ssem.at[i], ctx, rep).wait_send()
        g_copy(0, 0, 0, f_ssem.at[i], ctx, rep).wait_send()

    @pl.loop(0, pieces)
    def _(i):
        g_copy(0, 0, 0, h_ssem.at[i], ctx, rep).wait_send()

    swap.wait()
    out[xo] = o_recv[...]


def per_device(projected, short_taps, residues, decay_rates, skip_gain, out_weight):
    _, chans, length = projected.shape
    groups = chans // 128
    rows, feats = out_weight.shape
    half = feats // X
    pieces = chans // KC
    par = jnp.concatenate(
        [
            short_taps.transpose(0, 2, 1).reshape(9, chans),
            skip_gain[None],
            jnp.zeros((6, chans), F32),
        ],
        axis=0,
    )
    rates_t = decay_rates.T
    rate_tiles = rates_t.reshape(2, 8, groups, 128).transpose(0, 2, 1, 3).reshape(Z, 8, 128)
    fwd, bwd = tables(length)
    vm = pltpu.VMEM
    dma = pltpu.SemaphoreType.DMA
    out = pl.pallas_call(
        kernel,
        out_shape=jax.ShapeDtypeStruct((X, length, half), BF16),
        in_specs=[pl.BlockSpec(memory_space=vm)] * 8,
        out_specs=pl.BlockSpec(memory_space=vm),
        scratch_shapes=[
            vm((3, length + 8, chans), F32),
            vm((8, chans), F32),
            vm((8, chans), F32),
            vm((length, chans), F32),
            vm((length, chans), F32),
            vm((2 * length, chans), F32),
            vm((length, chans), F32),
            vm((Z, 8, 128), F32),
            vm((Z, 8, 128), F32),
            vm((8, 128), F32),
            vm((X * Y, 8, 128), F32),
            vm((Z, 8, 128), F32),
            vm((Z, 8, 128), F32),
            vm((X, REPS, pieces, length, KC), BF16),
            vm((X * Y * Z * rows, half), BF16),
            vm((X * length, half), F32),
            vm((length, half), BF16),
            vm((length, half), BF16),
            dma((2,)),
            dma((Z,)),
            dma((Z,)),
            dma((X * Y,)),
            dma((X * Y,)),
            dma((Z,)),
            dma((Z,)),
            dma((X * Y * Z,)),
            dma((2,)),
            dma(((Y - 1) * (Z + 1),)),
            dma(((1 + Y) * 2 * (Z // 2),)),
            dma((X * REPS * pieces,)),
            dma((3 * pieces,)),
            dma((3 * pieces,)),
            dma((pieces,)),
            dma((2,)),
        ],
        compiler_params=pltpu.CompilerParams(
            collective_id=0, has_side_effects=True, vmem_limit_bytes=40 * 1024 * 1024
        ),
        name="hyena",
    )(
        projected, par, rates_t[:, None, :], residues.T[:, None, :], rate_tiles,
        jnp.asarray(fwd), jnp.asarray(bwd), out_weight,
    )
    return out.transpose(0, 2, 1).reshape(feats, length)


def solution(mesh):
    in_specs = (
        P(None, "rep", "ctx"),
        P(None, "rep", None),
        P("rep", None),
        P("rep", None),
        P("rep"),
        P("ctx", "rep"),
    )
    out_specs = P("rep", "ctx")
    return jax.shard_map(
        per_device, mesh=mesh, in_specs=in_specs, out_specs=out_specs, check_vma=False
    )
```

time: 780 us -> 85.1 us (0.11)
  the two profiles are of different devices: /device:TPU:4 before, /device:TPU:2 now
where the time goes in v1:
time: 85.1 us; the launch traced here: 84.8 us
  Pallas kernels  80.1 us (94%)
  local copies, waits for them, and re-layouts  4.58 us (5%)
    pallas_call x1, Pallas kernels, per_device(): pl.pallas_call(kernel, out_shape=jax.ShapeDtypeStruct((X, length, half),...  80.1 us
    unnamed x14, local copies, waits for them, and re-layouts  2.72 us

profile of v1, /device:TPU:2, one launch (start us, length us, event | category | flops | bytes accessed | tf_op | source)
XLA Modules:
  0.0 84.8 jit_solution(10603589605762552257)
XLA Ops:
  0.0 0.1 pad.2.clone
  0.1 0.0 copy-start.6
  0.1 0.0 copy-start.5
  0.1 0.8 %reshape.12 = f32[9,1024]{1,0:T(8,128)S(1)} reshape(f32[3,3,1024]{2,1,0:T(4,128)} %bitcast.16) | data formatting | bytes 73728 | tf_op jit(solution)/shard_map/reshape | solution.py:463
  0.9 0.0 copy-done.6
  0.9 0.0 copy-start.3
  1.0 0.1 maximum_maximum_fusion.par
  1.0 0.0 copy-done.5
  1.0 0.0 copy-start.1
  1.0 0.0 copy-start.2
  1.1 0.8 copy-done.1
  1.9 0.0 copy-start.4
  1.9 0.0 copy-done.3
  1.9 0.0 copy-done.2
  2.0 0.7 copy-done.4
  2.7 0.0 copy-start
  2.7 1.1 %copy-done = bf16[3,1024,128]{2,1,0:T(8,128)(2,1)S(1)} copy-done((bf16[3,1024,128]{2,1,0:T(8,128)(2,1)S(1)}, bf16[3,1024,128]{2,1,0:T(8,128)(2,1)}, u32[]{:S(2)}) %copy-start) | copy-done | bytes 786456
  3.9 80.1 %hyena.1 = bf16[2,128,512]{2,1,0:T(8,128)(2,1)S(1)} custom-call(bf16[3,1024,128]{2,1,0:T(8,128)(2,1)S(1)} %copy-done, f32[16,1024]{1,0:T(8,128)S(1)} %maximum_maximum_fusion.par, f32[16,1,1024]{2,1,0:T(1,128)S(1)} %broadcast_in_dim.14.rates3, f32[16,1,1024]{2,1,0:T(1,128)S(1)} %broadcast_in_dim.15.amps3, f32[16,8,128]{2,1,0:T(8,128)S(1)} %bitcast.14, ...), custom_call_target="tpu_custom_call" | custom-call | tf_op jit(solution)/shard_map/hyena/pallas_call | solution.py:474
  84.0 0.8 copy.9
  (3 shorter events, 0.1 us)
Async XLA Ops:
  0.1 0.9 %copy-start.6 = (f32[1024]{0:T(1024)S(1)}, f32[1024]{0:T(1024)}, u32[]{:S(2)}) copy-start(f32[1024]{0:T(1024)} %param.12) | copy-start | bytes 12292
  0.1 1.0 %copy-start.5 = (f32[1024,16]{0,1:T(8,128)S(1)}, f32[1024,16]{0,1:T(8,128)}, u32[]{:S(2)}) copy-start(f32[1024,16]{0,1:T(8,128)} %param.10) | copy-start | bytes 196612
  0.9 1.0 %copy-start.3 = (f32[256,128]{1,0:T(8,128)S(1)}, f32[256,128]{1,0:T(8,128)}, u32[]{:S(2)}) copy-start(f32[256,128]{1,0:T(8,128)} %constant.6.clone.fwd) | copy-start | bytes 393220
  1.0 0.8 copy-start.1
  1.0 0.9 %copy-start.2 = (f32[128,256]{1,0:T(8,128)S(1)}, f32[128,256]{1,0:T(8,128)}, u32[]{:S(2)}) copy-start(f32[128,256]{1,0:T(8,128)} %constant.7.clone.bwd) | copy-start | bytes 393220
  1.9 0.9 %copy-start.4 = (bf16[32,1024]{1,0:T(8,128)(2,1)S(1)}, bf16[32,1024]{1,0:T(8,128)(2,1)}, u32[]{:S(2)}) copy-start(bf16[32,1024]{1,0:T(8,128)(2,1)} %w_shard.1) | copy-start | bytes 196612
  2.7 1.1 %copy-start = (bf16[3,1024,128]{2,1,0:T(8,128)(2,1)S(1)}, bf16[3,1024,128]{2,1,0:T(8,128)(2,1)}, u32[]{:S(2)}) copy-start(bf16[3,1024,128]{2,1,0:T(8,128)(2,1)} %proj.1) | copy-start | bytes 2359300

commit v2 on v1

v2 whole, which is shorter than its diff:
```python
import math

import numpy as np
import jax
import jax.numpy as jnp
from jax import lax
from jax.experimental import pallas as pl
from jax.experimental.pallas import tpu as pltpu
from jax.sharding import PartitionSpec as P

X, Y, Z = 2, 4, 16
ZL = 4
REPS = 4
MODES = 16
KC = 256
F32 = jnp.float32
BF16 = jnp.bfloat16


def split(value):
    high = value.astype(BF16)
    return high, (value - high.astype(F32)).astype(BF16)


def tables(length):
    k = np.arange(length)[:, None]
    t = np.arange(length)[None, :]
    angle = math.pi * ((2 * k + 1) * t % (4 * length)) / (2 * length)
    forward = np.concatenate([np.cos(angle), -np.sin(angle)], axis=0).astype(np.float32)
    backward = (forward.T / length).astype(np.float32)

    def halves(table):
        high = table.astype(jnp.bfloat16)
        return high, (table - high.astype(np.float32)).astype(jnp.bfloat16)

    return np.concatenate(halves(forward), axis=1), np.concatenate(halves(backward), axis=0)


def kernel(
    proj_hbm, taps_hbm, amps_hbm, rates_hbm, skip, fwd, bwd, w_shard, out,
    proj, taps, amps, rates, ex, rev, first, ratio, wide, carry_w, rate_tiles,
    xs, halo_s, halo_r, prod, gate, local, s_send, s_recv, t_send, t_recv, starts, p_send, p_recv,
    gall, wg, acc, o_send, o_recv,
    word_sem, in_sem, halo_sem, s_ssem, s_rsem, t_ssem, t_rsem, p_ssem, p_rsem,
    wx_sem, wz_rsem, wz_ssem, wl_rsem, wr_rsem, wy_ssem, wh_rsem, wh_ssem, g_rsem, g_ssem, f_ssem, h_ssem, o_sem,
):
    chans, length = proj.shape[1], proj.shape[2]
    groups = chans // 128
    rows = w_shard.shape[0]
    half = w_shard.shape[1] // 2
    pieces = chans // KC
    steps = length // 8

    ctx = lax.axis_index("ctx")
    rep = lax.axis_index("rep")
    z = lax.rem(ctx, Z)
    y = lax.rem(ctx // Z, Y)
    xl = ctx // (Y * Z)
    xo = 1 - xl
    rep_core = rep + 1 - 2 * lax.rem(rep, 2)
    rep_far = rep + 2 - 4 * (rep // 2)

    def at(x_, y_, z_):
        return (x_ * Y + y_) * Z + z_

    def remote(src, dst, ssem, rsem, c, r=None):
        return pltpu.make_async_remote_copy(
            src_ref=src, dst_ref=dst, send_sem=ssem, recv_sem=rsem,
            device_id=(c, rep if r is None else r), device_id_type=pl.DeviceIdType.MESH,
        )

    nxt = lax.rem(ctx + 1, X * Y * Z)
    prv = lax.rem(ctx + X * Y * Z - 1, X * Y * Z)
    zr = at(xl, y, lax.rem(z + 1, Z))
    zl = at(xl, y, lax.rem(z + Z - 1, Z))

    bar = pltpu.get_barrier_semaphore()

    def hello(c, r):
        pl.semaphore_signal(bar, inc=1, device_id=(c, r), device_id_type=pl.DeviceIdType.MESH)

    ZH = Z // ZL
    zh = z // ZL
    plane = Y * ZL
    mine = y * ZL + lax.rem(z, ZL)
    slab = xl * ZH + zh

    def plane_peer(q):
        return at(xl, q // ZL, zh * ZL + lax.rem(q, ZL))

    def slab_peer(h):
        return at(h // ZH, y, lax.rem(h, ZH) * ZL + lax.rem(z, ZL))

    up = at(xl, y, lax.rem(z + ZL, Z))
    down = at(xl, y, lax.rem(z + Z - ZL, Z))
    cx = at(xo, y, z)

    @pl.loop(1, plane)
    def _(d):
        hello(plane_peer(lax.rem(mine + d, plane)), rep)

    for c in (nxt, prv, zr, zl, up, down, cx):
        hello(c, rep)
    hello(ctx, rep_core)
    hello(cx, rep_far)
    reads = [
        pltpu.make_async_copy(proj_hbm.at[i], proj.at[i], in_sem.at[i]) for i in range(3)
    ]
    reads += [
        pltpu.make_async_copy(rates_hbm, rates, in_sem.at[3]),
        pltpu.make_async_copy(amps_hbm, amps, in_sem.at[4]),
        pltpu.make_async_copy(taps_hbm, taps, in_sem.at[5]),
    ]
    for read in reads:
        read.start()

    def lanes(g, width=128):
        return pl.ds(pl.multiple_of(g * width, width), width)

    eye = (
        lax.broadcasted_iota(jnp.int32, (length, length), 0)
        == lax.broadcasted_iota(jnp.int32, (length, length), 1)
    ).astype(BF16)

    for s in range(3):
        reads[s].wait()

        @pl.loop(0, groups)
        def _(g):
            xs[s, pl.ds(8, length), lanes(g)] = lax.dot_general(
                eye, proj[s, lanes(g), :], (((1,), (1,)), ((), ())), preferred_element_type=F32
            )

        xs[s, pl.ds(0, 8), :] = jnp.zeros((8, chans), F32)
    halo_s[...] = jnp.zeros_like(halo_s)
    for s in range(3):
        halo_s[pl.ds(2 * s, 2), :] = xs[s, pl.ds(8 + length - 2, 2), :]

    pl.semaphore_wait(bar, (plane - 1) + 7 + 2)

    def pass_on(i):
        for c in (up, down):
            pl.semaphore_signal(
                word_sem.at[i], inc=1, device_id=(c, rep), device_id_type=pl.DeviceIdType.MESH
            )

    pass_on(0)
    halo = remote(halo_s, halo_r, halo_sem.at[0], halo_sem.at[1], nxt)
    halo.start()

    RZ = Z // 2
    half_rows = rows // 2

    def wcols(i):
        return w_shard.at[:, pl.ds(pl.multiple_of(i * half, half), half)]

    x_copy = remote(wcols(xo), wg.at[xl, y, z], wx_sem.at[0], wx_sem.at[1], cx)
    x_copy.start()
    own = pltpu.make_async_copy(wcols(xl), wg.at[xl, y, z], wx_sem.at[2])
    own.start()

    def y_of(d):
        return lax.rem(y + d, Y)

    def z_of(d):
        return lax.rem(z + d + Z, Z)

    y_next, y_prev = at(xl, y_of(1), z), at(xl, y_of(Y - 1), z)

    def w_half(d_y, d_z, i, ssem, rsem, c):
        part = wg.at[:, y_of(d_y), z_of(d_z), pl.ds(i * half_rows, half_rows)]
        return remote(part, part, ssem, rsem.at[i * Z + z_of(d_z)], c)

    def w_round(d_z, i, right, k):
        ssem = wz_ssem.at[(i * 2 + right) * RZ + k]
        return w_half(0, d_z, i, ssem, wz_rsem, zr if right else zl)

    def w_arrived(d_z, i):
        w_half(0, d_z, i, wx_sem.at[0], wz_rsem, ctx).wait_recv()

    def w_whole(d_y, d_z, ssem, rsem, c):
        part = wg.at[:, y_of(d_y), z_of(d_z)]
        return remote(part, part, ssem, rsem.at[z_of(d_z)], c)

    def w_spread(d_z):
        w_whole(0, d_z, wy_ssem.at[z_of(d_z)], wl_rsem, y_next).start()
        w_whole(0, d_z, wy_ssem.at[Z + z_of(d_z)], wr_rsem, y_prev).start()

    def w_relay(d_z):
        w_whole(Y - 1, d_z, wx_sem.at[0], wl_rsem, ctx).wait_recv()
        w_half(Y - 1, d_z, 0, wh_ssem.at[z_of(d_z)], wh_rsem, y_next).start()
        w_whole(1, d_z, wx_sem.at[0], wr_rsem, ctx).wait_recv()
        w_half(1, d_z, 1, wh_ssem.at[Z + z_of(d_z)], wh_rsem, y_prev).start()

    def w_relayed(d_z):
        for i in range(2):
            w_half(2, d_z, i, wx_sem.at[0], wh_rsem, ctx).wait_recv()

    def w_start():
        own.wait()
        x_copy.wait_recv()
        for i in range(2):
            w_round(0, i, 1, 0).start()
            w_round(0, i, 0, 0).start()
        w_spread(0)

    def w_step(k):
        if k >= RZ:
            return
        for i in range(2):
            w_arrived(-k, i)
            if k < RZ - 1 or i == 0:
                w_round(-k, i, 1, k).start()
            w_arrived(k, i)
            if k < RZ - 1 or i == 1:
                w_round(k, i, 0, k).start()
        w_spread(-k)
        w_spread(k)
        w_relay(1 - k)
        if k > 1:
            w_relay(k - 1)

    def w_last():
        for i in range(2):
            w_arrived(RZ, i)
        w_spread(RZ)
        w_relay(1 - RZ)
        if RZ > 1:
            w_relay(RZ - 1)

    sub = lax.broadcasted_iota(jnp.int32, (MODES, 8, 128), 1).astype(F32)
    for read in reads[3:]:
        read.wait()

    @pl.loop(0, groups)
    def _(g):
        r2 = rates[:, lanes(g)]
        w2 = amps[:, lanes(g)] * jnp.sqrt(2.0 * r2)
        rate_tiles[g] = r2[0:8]
        rate_tiles[groups + g] = r2[8:16]
        once = w2 * jnp.exp(-r2)
        carry_w[g] = once[0:8]
        carry_w[groups + g] = once[8:16]
        r = r2[:, None, :]
        ex[:, :, lanes(g)] = jnp.exp(-r * sub)
        back = jnp.exp(-r * (7.0 - sub))
        rev[:, :, lanes(g)] = back
        first[:, :, lanes(g)] = back * jnp.exp(-float(length - 8) * r)
        ratio[:, :, lanes(g)] = jnp.exp(-8.0 * r)
        wide[:, :, lanes(g)] = w2[:, None, :]

    w_start()

    def featured(g, begin, count):
        made = []
        for s in range(3):
            total = taps[s, pl.ds(0, 1), lanes(g)] * xs[s, pl.ds(8 + begin, count), lanes(g)]
            for j in range(1, 3):
                total = total + (
                    taps[s, pl.ds(j, 1), lanes(g)]
                    * xs[s, pl.ds(8 + begin - j, count), lanes(g)]
                )
            made.append(total)
        return made[0].astype(BF16).astype(F32), (made[1] * made[2]).astype(BF16).astype(F32)

    top = lax.broadcasted_iota(jnp.int32, (8, 128), 0) < 2

    @pl.loop(0, groups)
    def _(g):
        gate_here, prod_here = featured(g, 0, length)
        gate[:, lanes(g)] = gate_here
        prod[:, lanes(g)] = prod_here
        step = ratio[:, :, lanes(g)]
        state = jnp.where(top, 0.0, prod[pl.ds(0, 8), lanes(g)])[None] * step
        for a in range(1, steps):
            state = state + prod[pl.ds(8 * a, 8), lanes(g)][None]
            if a < steps - 1:
                state = state * step
        ends = jnp.sum(state * rev[:, :, lanes(g)], axis=1)
        s_send[g] = ends[0:8]
        s_send[groups + g] = ends[8:16]

    halo.wait_recv()
    keep = jnp.where(ctx > 0, 1.0, 0.0).astype(F32)
    for s in range(3):
        xs[s, pl.ds(6, 2), :] = halo_r[pl.ds(2 * s, 2), :] * keep

    @pl.loop(0, groups)
    def _(g):
        gate_here, prod_here = featured(g, 0, 8)
        gate[pl.ds(0, 8), lanes(g)] = gate_here
        prod[pl.ds(0, 8), lanes(g)] = prod_here
        more = jnp.sum(
            first[:, :, lanes(g)] * jnp.where(top, prod_here, 0.0)[None], axis=1
        )
        s_send[g] += more[0:8]
        s_send[groups + g] += more[8:16]

    pl.semaphore_wait(word_sem.at[0], 2)
    pass_on(1)
    s_recv[mine] = s_send[mine]

    @pl.loop(1, plane)
    def _(d):
        to = lax.rem(mine + d, plane)
        remote(
            s_send.at[to], s_recv.at[mine], s_ssem.at[d], s_rsem.at[mine], plane_peer(to)
        ).start()

    w_step(1)

    @pl.loop(0, groups)
    def _(g):
        q = wide[:, :, lanes(g)] * ex[:, :, lanes(g)]
        step = ratio[:, :, lanes(g)]
        for a in range(steps):
            local[pl.ds(8 * a, 8), lanes(g)] = jnp.sum(q, axis=0)
            q = q * step

    def dot(left, right):
        return jnp.dot(left, right, preferred_element_type=F32)

    @pl.loop(0, chans // 256)
    def _(g):
        h_hi, h_lo = split(local[:, lanes(g, 256)])
        h_spec = dot(fwd[...], jnp.concatenate([h_hi, h_hi], axis=0)) + dot(fwd[:, :length], h_lo)
        u = prod[:, lanes(g, 256)]
        u_hi = u.astype(BF16)
        u_spec = dot(fwd[...], jnp.concatenate([u_hi, u_hi], axis=0))
        u_re, u_im = u_spec[:length], u_spec[length:]
        h_re, h_im = h_spec[:length], h_spec[length:]
        joint = jnp.concatenate(
            [u_re * h_re - u_im * h_im, u_re * h_im + u_im * h_re], axis=0
        )
        j_hi, j_lo = split(joint)
        mixed = dot(bwd[...], j_hi)
        mixed = mixed[:length] + mixed[length:] + dot(bwd[:length, :], j_lo)
        local[:, lanes(g, 256)] = mixed + skip[:, lanes(g, 256)] * u

    w_step(2)

    @pl.loop(1, plane)
    def _(d):
        src = lax.rem(mine + d, plane)
        remote(s_send.at[mine], s_recv.at[src], s_ssem.at[d], s_rsem.at[src], ctx).wait_recv()

    tile_rate = rate_tiles[mine]
    block_decay = jnp.exp(-float(length) * tile_rate)
    for i in range(Y):
        total = jnp.zeros((8, 128), F32)
        for j in range(ZL):
            total = total * block_decay + s_recv[i * ZL + j]
        t_send[i] = total
        t_recv[slab, i] = total
    pl.semaphore_wait(word_sem.at[1], 2)

    @pl.loop(1, X * ZH)
    def _(d):
        to = slab_peer(lax.rem(slab + d, X * ZH))
        remote(t_send, t_recv.at[slab], t_ssem.at[d], t_rsem.at[slab], to).start()

    w_step(3)
    w_step(4)

    @pl.loop(1, X * ZH)
    def _(d):
        src = lax.rem(slab + d, X * ZH)
        remote(t_send, t_recv.at[src], t_ssem.at[d], t_rsem.at[src], ctx).wait_recv()

    group_decay = jnp.exp(-float(length * ZL) * tile_rate)
    carry = jnp.zeros((8, 128), F32)
    for i in range(X):
        for j in range(Y):
            for k in range(ZH):
                starts[(i * Y + j) * ZH + k] = carry
                carry = carry * group_decay + t_recv[i * ZH + k, j]
    for i in range(Y):
        carry = starts[(xl * Y + i) * ZH + zh]
        for j in range(ZL):
            p_send[i * ZL + j] = carry
            carry = carry * block_decay + s_recv[i * ZL + j]
    p_recv[mine] = p_send[mine]

    @pl.loop(1, plane)
    def _(d):
        to = lax.rem(mine + d, plane)
        remote(
            p_send.at[to], p_recv.at[mine], p_ssem.at[d], p_rsem.at[mine], plane_peer(to)
        ).start()

    w_step(5)
    w_step(6)

    @pl.loop(1, plane)
    def _(d):
        src = lax.rem(mine + d, plane)
        remote(p_send.at[mine], p_recv.at[src], p_ssem.at[d], p_rsem.at[src], ctx).wait_recv()

    def piece(x_, r_, k):
        return gall.at[r_, k, pl.ds(pl.multiple_of(x_ * length, length), length), :]

    def g_copy(x_, r_, k, ssem, c, r):
        return remote(
            piece(x_, r_, k), piece(x_, r_, k), ssem, g_rsem.at[(x_ * REPS + r_) * pieces + k], c, r
        )

    def g_arrived(x_, r_, k):
        g_copy(x_, r_, k, g_ssem.at[0], ctx, rep).wait_recv()

    per = KC // 128

    def finish(k):
        for i in range(per):
            g = k * per + i
            before = jnp.concatenate(
                [p_recv[g] * carry_w[g], p_recv[groups + g] * carry_w[groups + g]], axis=0
            )
            q = before[:, None, :] * ex[:, :, lanes(g)]
            step = ratio[:, :, lanes(g)]
            for a in range(steps):
                here = (pl.ds(8 * a, 8), lanes(g))
                local[here] = local[here] + jnp.sum(q, axis=0)
                q = q * step
            long = local[:, lanes(g)].astype(BF16).astype(F32)
            gall[rep, k, pl.ds(pl.multiple_of(xl * length, length), length), pl.ds(128 * i, 128)] = (
                gate[:, lanes(g)] * long
            ).astype(BF16)

    @pl.loop(0, pieces)
    def _(k):
        finish(k)
        g_copy(xl, rep, k, g_ssem.at[3 * k], ctx, rep_core).start()
        g_copy(xl, rep, k, g_ssem.at[3 * k + 1], cx, rep).start()
        g_copy(xl, rep, k, g_ssem.at[3 * k + 2], cx, rep_far).start()

    def g_pass(k):
        g_arrived(xo, rep, k)
        if k % 2 == 0:
            g_copy(xo, rep, k, h_ssem.at[k], cx, rep_far).start()
        g_copy(xo, rep, k, f_ssem.at[3 * k], ctx, rep_core).start()
        g_arrived(xo, rep_far, k)
        if k % 2 == 1:
            g_copy(xo, rep_far, k, h_ssem.at[k], cx, rep).start()
        g_copy(xo, rep_far, k, f_ssem.at[3 * k + 1], ctx, rep_core).start()

    w_step(7)
    for k in range(pieces // 2):
        g_pass(k)
    w_last()
    for k in range(pieces // 2, pieces):
        g_pass(k)
    w_relay(RZ)

    @pl.loop(0, Z)
    def _(d):
        w_relayed(d)

    def project(r_, k):
        n = (r_ * pieces + k) * (KC // rows)
        part = wg[n // (Y * Z), lax.rem(n // Z, Y), pl.ds(lax.rem(n, Z), KC // rows)]
        acc[...] += jnp.dot(gall[r_, k], part.reshape(KC, half), preferred_element_type=F32)

    acc[...] = jnp.zeros_like(acc)

    @pl.loop(0, pieces)
    def _(k):
        project(rep, k)
        g_arrived(xl, rep_far, k)
        g_copy(xl, rep_far, k, f_ssem.at[3 * k + 2], ctx, rep_core).start()

    @pl.loop(0, pieces)
    def _(k):
        project(rep_far, k)

    for src_rep in (rep_core, rep_far + rep_core - rep):
        @pl.loop(0, pieces)
        def _(k):
            g_arrived(xl, src_rep, k)
            g_arrived(xo, src_rep, k)
            project(src_rep, k)

    o_send[...] = acc[pl.ds(pl.multiple_of(xo * length, length), length), :].astype(BF16)
    swap = remote(o_send, o_recv, o_sem.at[0], o_sem.at[1], cx)
    swap.start()
    out[xl] = acc[pl.ds(pl.multiple_of(xl * length, length), length), :].astype(BF16)

    halo.wait_send()
    x_copy.wait_send()

    @pl.loop(1, plane)
    def _(d):
        remote(s_send.at[0], s_recv.at[0], s_ssem.at[d], s_rsem.at[0], ctx).wait_send()
        remote(p_send.at[0], p_recv.at[0], p_ssem.at[d], p_rsem.at[0], ctx).wait_send()

    @pl.loop(1, X * ZH)
    def _(d):
        remote(t_send, t_recv.at[0], t_ssem.at[d], t_rsem.at[0], ctx).wait_send()

    @pl.loop(0, Z)
    def _(i):
        for j in range(2):
            w_whole(0, 0, wy_ssem.at[j * Z + i], wl_rsem, ctx).wait_send()
            w_half(0, 0, 0, wh_ssem.at[j * Z + i], wh_rsem, ctx).wait_send()

    for k in range(RZ):
        for i in range(2):
            for right in range(2):
                if k < RZ - 1 or i != right:
                    w_round(0, i, right, k).wait_send()

    @pl.loop(0, 3 * pieces)
    def _(i):
        g_copy(0, 0, 0, g_ssem.at[i], ctx, rep).wait_send()
        g_copy(0, 0, 0, f_ssem.at[i], ctx, rep).wait_send()

    @pl.loop(0, pieces)
    def _(i):
        g_copy(0, 0, 0, h_ssem.at[i], ctx, rep).wait_send()

    swap.wait()
    out[xo] = o_recv[...]


def per_device(projected, short_taps, residues, decay_rates, skip_gain, out_weight):
    _, chans, length = projected.shape
    groups = chans // 128
    rows, feats = out_weight.shape
    half = feats // X
    pieces = chans // KC
    fwd, bwd = tables(length)
    vm = pltpu.VMEM
    dma = pltpu.SemaphoreType.DMA
    out = pl.pallas_call(
        kernel,
        out_shape=jax.ShapeDtypeStruct((X, length, half), BF16),
        in_specs=[pl.BlockSpec(memory_space=pltpu.HBM)] * 4
        + [pl.BlockSpec(memory_space=vm)] * 3
        + [pl.BlockSpec(memory_space=pltpu.HBM)],
        out_specs=pl.BlockSpec(memory_space=vm),
        scratch_shapes=[
            vm((3, chans, length), BF16),
            vm((3, 3, chans), F32),
            vm((MODES, chans), F32),
            vm((MODES, chans), F32),
            vm((MODES, 8, chans), F32),
            vm((MODES, 8, chans), F32),
            vm((MODES, 8, chans), F32),
            vm((MODES, 1, chans), F32),
            vm((MODES, 1, chans), F32),
            vm((Y * ZL, 8, 128), F32),
            vm((Y * ZL, 8, 128), F32),
            vm((3, length + 8, chans), F32),
            vm((8, chans), F32),
            vm((8, chans), F32),
            vm((length, chans), F32),
            vm((length, chans), F32),
            vm((length, chans), F32),
            vm((Y * ZL, 8, 128), F32),
            vm((Y * ZL, 8, 128), F32),
            vm((Y, 8, 128), F32),
            vm((X * Z // ZL, Y, 8, 128), F32),
            vm((X * Y * Z // ZL, 8, 128), F32),
            vm((Y * ZL, 8, 128), F32),
            vm((Y * ZL, 8, 128), F32),
            vm((REPS, pieces, X * length, KC), BF16),
            vm((X, Y, Z, rows, half), BF16),
            vm((X * length, half), F32),
            vm((length, half), BF16),
            vm((length, half), BF16),
            pltpu.SemaphoreType.REGULAR((2,)),
            dma((6,)),
            dma((2,)),
            dma((Y * ZL,)),
            dma((Y * ZL,)),
            dma((X * Z // ZL,)),
            dma((X * Z // ZL,)),
            dma((Y * ZL,)),
            dma((Y * ZL,)),
            dma((3,)),
            dma((2 * Z,)),
            dma((2 * Z,)),
            dma((Z,)),
            dma((Z,)),
            dma((2 * Z,)),
            dma((2 * Z,)),
            dma((2 * Z,)),
            dma((X * REPS * pieces,)),
            dma((3 * pieces,)),
            dma((3 * pieces,)),
            dma((pieces,)),
            dma((2,)),
        ],
        compiler_params=pltpu.CompilerParams(
            collective_id=0, has_side_effects=True, vmem_limit_bytes=60 * 1024 * 1024
        ),
        name="hyena",
    )(
        projected, short_taps.transpose(0, 2, 1), residues.T, decay_rates.T, skip_gain[None],
        jnp.asarray(fwd), jnp.asarray(bwd), out_weight,
    )
    return out.transpose(0, 2, 1).reshape(feats, length)


def solution(mesh):
    in_specs = (
        P(None, "rep", "ctx"),
        P(None, "rep", None),
        P("rep", None),
        P("rep", None),
        P("rep"),
        P("ctx", "rep"),
    )
    out_specs = P("rep", "ctx")
    return jax.shard_map(
        per_device, mesh=mesh, in_specs=in_specs, out_specs=out_specs, check_vma=False
    )
```

time: 85.1 us -> 72.8 us (0.86)
  the two profiles are of different devices: /device:TPU:2 before, /device:TPU:6 now
where the time goes in v2:
time: 72.8 us; the launch traced here: 72.5 us
  Pallas kernels  70.7 us (97%)
  local copies, waits for them, and re-layouts  1.79 us (2%)
    pallas_call x1, Pallas kernels, per_device(): pl.pallas_call(kernel, out_shape=jax.ShapeDtypeStruct((X, length, half),...  70.7 us
    transpose x1, local copies, waits for them, and re-layouts, per_device(): return out.transpose(0, 2, 1).reshape(feats, length)  1.79 us

profile of v2, /device:TPU:6, one launch (start us, length us, event | category | flops | bytes accessed | tf_op | source)
XLA Modules:
  0.0 72.5 jit_solution(2373653105039367517)
XLA Ops:
  0.0 70.7 %hyena.1 = bf16[2,128,512]{2,1,0:T(8,128)(2,1)} custom-call(bf16[3,1024,128]{2,1,0:T(8,128)(2,1)} %proj_hbm.1, f32[3,3,1024]{2,1,0:T(4,128)} %bitcast.9, f32[16,1024]{1,0:T(8,128)} %bitcast.7, f32[16,1024]{1,0:T(8,128)} %bitcast.8, f32[1,1024]{1,0:T(1,128)} %bitcast.10, bf16[256,256]{1,0:T(8,128)(2,1)} %constant.4.clone.fwd, ...), custom_call_target="tpu_custom_call" | custom-call | tf_op jit(solution)/shard_map/hyena/pallas_call | solution.py:533
  70.7 1.8 %copy.9 = bf16[2,512,128]{2,1,0:T(8,128)(2,1)} copy(bf16[2,512,128]{1,2,0:T(8,128)(2,1)} %bitcast.6) | data formatting | bytes 524288 | tf_op jit(solution)/shard_map/transpose | solution.py:601

commit v3 on v2

--- a/solution.py
+++ b/solution.py
@@ -39,10 +39,10 @@
 def kernel(
     proj_hbm, taps_hbm, amps_hbm, rates_hbm, skip, fwd, bwd, w_shard, out,
     proj, taps, amps, rates, ex, rev, first, ratio, wide, carry_w, rate_tiles,
-    xs, halo_s, halo_r, prod, gate, local, s_send, s_recv, t_send, t_recv, starts, p_send, p_recv,
-    gall, wg, acc, o_send, o_recv,
-    word_sem, in_sem, halo_sem, s_ssem, s_rsem, t_ssem, t_rsem, p_ssem, p_rsem,
-    wx_sem, wz_rsem, wz_ssem, wl_rsem, wr_rsem, wy_ssem, wh_rsem, wh_ssem, g_rsem, g_ssem, f_ssem, h_ssem, o_sem,
+    xs, halo_s, halo_r, prod, gate, local, s_send, s_recv, t_send, t_recv, starts, e_send, e_recv, p_send, p_recv,
+    gall, wg, acc, o_send, o_own,
+    word_sem, in_sem, halo_sem, s_ssem, s_rsem, t_ssem, t_rsem, e_ssem, e_rsem, p_ssem, p_rsem,
+    wx_sem, wf_rsem, wf_ssem, wb_rsem, wbz_ssem, wz_rsem, wz_ssem, wl_rsem, wr_rsem, wy_ssem, wh_rsem, wh_ssem, g_rsem, g_ssem, f_ssem, h_ssem, o_sem,
 ):
     chans, length = proj.shape[1], proj.shape[2]
     groups = chans // 128
@@ -83,13 +83,12 @@
     zh = z // ZL
     plane = Y * ZL
     mine = y * ZL + lax.rem(z, ZL)
-    slab = xl * ZH + zh
 
     def plane_peer(q):
         return at(xl, q // ZL, zh * ZL + lax.rem(q, ZL))
 
-    def slab_peer(h):
-        return at(h // ZH, y, lax.rem(h, ZH) * ZL + lax.rem(z, ZL))
+    def slab_peer(x_, h):
+        return at(x_, y, h * ZL + lax.rem(z, ZL))
 
     up = at(xl, y, lax.rem(z + ZL, Z))
     down = at(xl, y, lax.rem(z + Z - ZL, Z))
@@ -150,6 +149,8 @@
 
     RZ = Z // 2
     half_rows = rows // 2
+    last = half // 4 if half >= 512 else half // 2
+    lead, rest = pl.ds(0, half - last), pl.ds(half - last, last)
 
     def wcols(i):
         return w_shard.at[:, pl.ds(pl.multiple_of(i * half, half), half)]
@@ -168,7 +169,7 @@
     y_next, y_prev = at(xl, y_of(1), z), at(xl, y_of(Y - 1), z)
 
     def w_half(d_y, d_z, i, ssem, rsem, c):
-        part = wg.at[:, y_of(d_y), z_of(d_z), pl.ds(i * half_rows, half_rows)]
+        part = wg.at[:, y_of(d_y), z_of(d_z), pl.ds(i * half_rows, half_rows), lead]
         return remote(part, part, ssem, rsem.at[i * Z + z_of(d_z)], c)
 
     def w_round(d_z, i, right, k):
@@ -179,7 +180,7 @@
         w_half(0, d_z, i, wx_sem.at[0], wz_rsem, ctx).wait_recv()
 
     def w_whole(d_y, d_z, ssem, rsem, c):
-        part = wg.at[:, y_of(d_y), z_of(d_z)]
+        part = wg.at[:, y_of(d_y), z_of(d_z), :, lead]
         return remote(part, part, ssem, rsem.at[z_of(d_z)], c)
 
     def w_spread(d_z):
@@ -195,6 +196,33 @@
     def w_relayed(d_z):
         for i in range(2):
             w_half(2, d_z, i, wx_sem.at[0], wh_rsem, ctx).wait_recv()
+
+    def b_first(d_y, ssem, c):
+        part = wg.at[:, y_of(d_y), z, :, rest]
+        return remote(part, part, ssem, rsem=wf_rsem.at[y_of(d_y)], c=c)
+
+    def b_copy(p, d_z, ssem, c):
+        part = wg.at[:, pl.ds(p * (Y // 2), Y // 2), z_of(d_z), :, rest]
+        return remote(part, part, ssem, rsem=wb_rsem.at[p * Z + z_of(d_z)], c=c)
+
+    def b_round(p, d_z, right, k):
+        return b_copy(p, d_z, wbz_ssem.at[(p * 2 + right) * RZ + k], zr if right else zl)
+
+    def b_arrived(p, d_z):
+        b_copy(p, d_z, wx_sem.at[0], ctx).wait_recv()
+
+    def b_step(k):
+        for j in range(1, Y if k == 0 else 1):
+            b_first(j, wf_ssem.at[0], ctx).wait_recv()
+        for p in range(2):
+            if k > 0:
+                b_arrived(p, -k)
+            if k < RZ - 1 or p == 0:
+                b_round(p, -k, 1, k).start()
+            if k > 0:
+                b_arrived(p, k)
+            if k < RZ - 1 or p == 1:
+                b_round(p, k, 0, k).start()
 
     def w_start():
         own.wait()
@@ -202,6 +230,8 @@
         for i in range(2):
             w_round(0, i, 1, 0).start()
             w_round(0, i, 0, 0).start()
+        for j in range(1, Y):
+            b_first(0, wf_ssem.at[j], at(xl, y_of(j), z)).start()
         w_spread(0)
 
     def w_step(k):
@@ -216,17 +246,21 @@
                 w_round(k, i, 0, k).start()
         w_spread(-k)
         w_spread(k)
-        w_relay(1 - k)
+        b_step(k - 1)
         if k > 1:
-            w_relay(k - 1)
+            w_relay(2 - k)
+        if k > 2:
+            w_relay(k - 2)
 
     def w_last():
         for i in range(2):
             w_arrived(RZ, i)
         w_spread(RZ)
-        w_relay(1 - RZ)
-        if RZ > 1:
-            w_relay(RZ - 1)
+        b_step(RZ - 1)
+        for k in (RZ - 2, RZ - 1):
+            w_relay(-k)
+            if k > 0:
+                w_relay(k)
 
     sub = lax.broadcasted_iota(jnp.int32, (MODES, 8, 128), 1).astype(F32)
     for read in reads[3:]:
@@ -351,31 +385,49 @@
         for j in range(ZL):
             total = total * block_decay + s_recv[i * ZL + j]
         t_send[i] = total
-        t_recv[slab, i] = total
+        t_recv[zh, i] = total
+    group = float(length * ZL)
+    share = jnp.zeros((8, 128), F32)
+    for i in range(Y):
+        left = (Y * ZH - 1 - (i * ZH + zh)).astype(F32)
+        share = share + t_send[i] * jnp.exp(-(group * left) * tile_rate)
+    e_send[...] = share
     pl.semaphore_wait(word_sem.at[1], 2)
 
-    @pl.loop(1, X * ZH)
-    def _(d):
-        to = slab_peer(lax.rem(slab + d, X * ZH))
-        remote(t_send, t_recv.at[slab], t_ssem.at[d], t_rsem.at[slab], to).start()
+    @pl.loop(1, ZH)
+    def _(d):
+        to = lax.rem(zh + d, ZH)
+        remote(t_send, t_recv.at[zh], t_ssem.at[d], t_rsem.at[zh], slab_peer(xl, to)).start()
+
+    @pl.loop(0, ZH)
+    def _(h):
+        remote(e_send, e_recv.at[zh], e_ssem.at[h], e_rsem.at[zh], slab_peer(xo, h)).start()
 
     w_step(3)
     w_step(4)
 
-    @pl.loop(1, X * ZH)
-    def _(d):
-        src = lax.rem(slab + d, X * ZH)
+    @pl.loop(1, ZH)
+    def _(d):
+        src = lax.rem(zh + d, ZH)
         remote(t_send, t_recv.at[src], t_ssem.at[d], t_rsem.at[src], ctx).wait_recv()
 
-    group_decay = jnp.exp(-float(length * ZL) * tile_rate)
+    @pl.loop(0, ZH)
+    def _(h):
+        remote(e_send, e_recv.at[h], e_ssem.at[h], e_rsem.at[h], ctx).wait_recv()
+
+    group_decay = jnp.exp(-group * tile_rate)
     carry = jnp.zeros((8, 128), F32)
-    for i in range(X):
-        for j in range(Y):
-            for k in range(ZH):
-                starts[(i * Y + j) * ZH + k] = carry
-                carry = carry * group_decay + t_recv[i * ZH + k, j]
+    for j in range(Y):
+        for k in range(ZH):
+            starts[j * ZH + k] = carry
+            carry = carry * group_decay + t_recv[k, j]
+    later = jnp.zeros((8, 128), F32)
+    for k in range(ZH):
+        later = later + e_recv[k]
+    later = jnp.where(xl > 0, later, 0.0)
     for i in range(Y):
-        carry = starts[(xl * Y + i) * ZH + zh]
+        n = i * ZH + zh
+        carry = starts[n] + later * jnp.exp(-(group * n.astype(F32)) * tile_rate)
         for j in range(ZL):
             p_send[i * ZL + j] = carry
             carry = carry * block_decay + s_recv[i * ZL + j]
@@ -397,7 +449,9 @@
         remote(p_send.at[mine], p_recv.at[src], p_ssem.at[d], p_rsem.at[src], ctx).wait_recv()
 
     def piece(x_, r_, k):
-        return gall.at[r_, k, pl.ds(pl.multiple_of(x_ * length, length), length), :]
+        return gall.at[
+            r_, pl.ds(pl.multiple_of(x_ * length, length), length), pl.ds(k * KC, KC)
+        ]
 
     def g_copy(x_, r_, k, ssem, c, r):
         return remote(
@@ -422,12 +476,10 @@
                 local[here] = local[here] + jnp.sum(q, axis=0)
                 q = q * step
             long = local[:, lanes(g)].astype(BF16).astype(F32)
-            gall[rep, k, pl.ds(pl.multiple_of(xl * length, length), length), pl.ds(128 * i, 128)] = (
-                gate[:, lanes(g)] * long
-            ).astype(BF16)
-
-    @pl.loop(0, pieces)
-    def _(k):
+            here = pl.ds(pl.multiple_of(xl * length, length), length)
+            gall[rep, here, lanes(g)] = (gate[:, lanes(g)] * long).astype(BF16)
+
+    for k in range(pieces):
         finish(k)
         g_copy(xl, rep, k, g_ssem.at[3 * k], ctx, rep_core).start()
         g_copy(xl, rep, k, g_ssem.at[3 * k + 1], cx, rep).start()
@@ -449,40 +501,55 @@
     w_last()
     for k in range(pieces // 2, pieces):
         g_pass(k)
+    for p in range(2):
+        b_arrived(p, RZ)
     w_relay(RZ)
 
     @pl.loop(0, Z)
     def _(d):
         w_relayed(d)
 
-    def project(r_, k):
-        n = (r_ * pieces + k) * (KC // rows)
-        part = wg[n // (Y * Z), lax.rem(n // Z, Y), pl.ds(lax.rem(n, Z), KC // rows)]
-        acc[...] += jnp.dot(gall[r_, k], part.reshape(KC, half), preferred_element_type=F32)
-
-    acc[...] = jnp.zeros_like(acc)
+    def project(r_, here):
+        n = r_ * (chans // rows) // Z
+        part = wg[n // Y, pl.ds(lax.rem(n, Y), chans // rows // Z)].reshape(chans, half)
+        return jnp.dot(gall[r_, here, :], part, preferred_element_type=F32)
+
+    both = pl.ds(0, X * length)
+    acc[...] = project(rep, both)
 
     @pl.loop(0, pieces)
     def _(k):
-        project(rep, k)
         g_arrived(xl, rep_far, k)
         g_copy(xl, rep_far, k, f_ssem.at[3 * k + 2], ctx, rep_core).start()
 
+    acc[...] += project(rep_far, both)
+    core_far = rep_far + rep_core - rep
+
     @pl.loop(0, pieces)
     def _(k):
-        project(rep_far, k)
-
-    for src_rep in (rep_core, rep_far + rep_core - rep):
-        @pl.loop(0, pieces)
-        def _(k):
-            g_arrived(xl, src_rep, k)
-            g_arrived(xo, src_rep, k)
-            project(src_rep, k)
-
-    o_send[...] = acc[pl.ds(pl.multiple_of(xo * length, length), length), :].astype(BF16)
-    swap = remote(o_send, o_recv, o_sem.at[0], o_sem.at[1], cx)
+        for x_ in range(X):
+            g_arrived(x_, rep_core, k)
+
+    acc[...] += project(rep_core, both)
+
+    @pl.loop(0, pieces)
+    def _(k):
+        for x_ in range(X):
+            g_arrived(x_, core_far, k)
+
+    def turn(x_, to):
+        here = pl.ds(pl.multiple_of(x_ * length, length), length)
+        acc[here, :] += project(core_far, here)
+        for i in range(half // 128):
+            cols = pl.ds(128 * i, 128)
+            to[cols, :] = acc[here, cols].T.astype(BF16)
+
+    turn(xo, o_send)
+    swap = remote(o_send, out.at[xl], o_sem.at[0], o_sem.at[1], cx)
     swap.start()
-    out[xl] = acc[pl.ds(pl.multiple_of(xl * length, length), length), :].astype(BF16)
+    turn(xl, o_own)
+    keep_own = pltpu.make_async_copy(o_own, out.at[xl], o_sem.at[2])
+    keep_own.start()
 
     halo.wait_send()
     x_copy.wait_send()
@@ -492,9 +559,13 @@
         remote(s_send.at[0], s_recv.at[0], s_ssem.at[d], s_rsem.at[0], ctx).wait_send()
         remote(p_send.at[0], p_recv.at[0], p_ssem.at[d], p_rsem.at[0], ctx).wait_send()
 
-    @pl.loop(1, X * ZH)
+    @pl.loop(1, ZH)
     def _(d):
         remote(t_send, t_recv.at[0], t_ssem.at[d], t_rsem.at[0], ctx).wait_send()
+
+    @pl.loop(0, ZH)
+    def _(h):
+        remote(e_send, e_recv.at[0], e_ssem.at[h], e_rsem.at[0], ctx).wait_send()
 
     @pl.loop(0, Z)
     def _(i):
@@ -502,11 +573,14 @@
             w_whole(0, 0, wy_ssem.at[j * Z + i], wl_rsem, ctx).wait_send()
             w_half(0, 0, 0, wh_ssem.at[j * Z + i], wh_rsem, ctx).wait_send()
 
+    for j in range(1, Y):
+        b_first(0, wf_ssem.at[j], ctx).wait_send()
     for k in range(RZ):
         for i in range(2):
             for right in range(2):
                 if k < RZ - 1 or i != right:
                     w_round(0, i, right, k).wait_send()
+                    b_round(i, 0, right, k).wait_send()
 
     @pl.loop(0, 3 * pieces)
     def _(i):
@@ -517,8 +591,9 @@
     def _(i):
         g_copy(0, 0, 0, h_ssem.at[i], ctx, rep).wait_send()
 
-    swap.wait()
-    out[xo] = o_recv[...]
+    keep_own.wait()
+    swap.wait_send()
+    remote(o_send, out.at[xo], o_sem.at[0], o_sem.at[1], ctx).wait_recv()
 
 
 def per_device(projected, short_taps, residues, decay_rates, skip_gain, out_weight):
@@ -532,11 +607,11 @@
     dma = pltpu.SemaphoreType.DMA
     out = pl.pallas_call(
         kernel,
-        out_shape=jax.ShapeDtypeStruct((X, length, half), BF16),
+        out_shape=jax.ShapeDtypeStruct((X, half, length), BF16),
         in_specs=[pl.BlockSpec(memory_space=pltpu.HBM)] * 4
         + [pl.BlockSpec(memory_space=vm)] * 3
         + [pl.BlockSpec(memory_space=pltpu.HBM)],
-        out_specs=pl.BlockSpec(memory_space=vm),
+        out_specs=pl.BlockSpec(memory_space=pl.ANY),
         scratch_shapes=[
             vm((3, chans, length), BF16),
             vm((3, 3, chans), F32),
@@ -558,25 +633,33 @@
             vm((Y * ZL, 8, 128), F32),
             vm((Y * ZL, 8, 128), F32),
             vm((Y, 8, 128), F32),
-            vm((X * Z // ZL, Y, 8, 128), F32),
-            vm((X * Y * Z // ZL, 8, 128), F32),
+            vm((Z // ZL, Y, 8, 128), F32),
+            vm((Y * Z // ZL, 8, 128), F32),
+            vm((8, 128), F32),
+            vm((Z // ZL, 8, 128), F32),
             vm((Y * ZL, 8, 128), F32),
             vm((Y * ZL, 8, 128), F32),
-            vm((REPS, pieces, X * length, KC), BF16),
+            vm((REPS, X * length, chans), BF16),
             vm((X, Y, Z, rows, half), BF16),
             vm((X * length, half), F32),
-            vm((length, half), BF16),
-            vm((length, half), BF16),
+            vm((half, length), BF16),
+            vm((half, length), BF16),
             pltpu.SemaphoreType.REGULAR((2,)),
             dma((6,)),
             dma((2,)),
             dma((Y * ZL,)),
             dma((Y * ZL,)),
-            dma((X * Z // ZL,)),
-            dma((X * Z // ZL,)),
+            dma((Z // ZL,)),
+            dma((Z // ZL,)),
+            dma((Z // ZL,)),
+            dma((Z // ZL,)),
             dma((Y * ZL,)),
             dma((Y * ZL,)),
             dma((3,)),
+            dma((Y,)),
+            dma((Y,)),
+            dma((2 * Z,)),
+            dma((2 * Z,)),
             dma((2 * Z,)),
             dma((2 * Z,)),
             dma((Z,)),
@@ -588,7 +671,7 @@
             dma((3 * pieces,)),
             dma((3 * pieces,)),
             dma((pieces,)),
-            dma((2,)),
+            dma((3,)),
         ],
         compiler_params=pltpu.CompilerParams(
             collective_id=0, has_side_effects=True, vmem_limit_bytes=60 * 1024 * 1024
@@ -598,7 +681,7 @@
         projected, short_taps.transpose(0, 2, 1), residues.T, decay_rates.T, skip_gain[None],
         jnp.asarray(fwd), jnp.asarray(bwd), out_weight,
     )
-    return out.transpose(0, 2, 1).reshape(feats, length)
+    return out.reshape(feats, length)
 
 
 def solution(mesh):

time: 72.8 us -> 70.6 us (0.970)
  the two profiles are of different devices: /device:TPU:6 before, /device:TPU:1 now
where the time goes in v3:
time: 70.6 us; the launch traced here: 70.4 us
  Pallas kernels  68.7 us (97%)
  local copies, waits for them, and re-layouts  1.67 us (2%)
    pallas_call x1, Pallas kernels, per_device(): pl.pallas_call(kernel, out_shape=jax.ShapeDtypeStruct((X, half, length),...  68.7 us
    unnamed x1, local copies, waits for them, and re-layouts  1.67 us

profile of v3, /device:TPU:1, one launch (start us, length us, event | category | flops | bytes accessed | tf_op | source)
XLA Modules:
  0.0 70.4 jit_solution(1814236189442262651)
XLA Ops:
  0.0 68.7 %hyena.1 = bf16[2,512,128]{2,1,0:T(8,128)(2,1)} custom-call(bf16[3,1024,128]{2,1,0:T(8,128)(2,1)} %proj_hbm.1, f32[3,3,1024]{2,1,0:T(4,128)} %bitcast.8, f32[16,1024]{1,0:T(8,128)} %bitcast.6, f32[16,1024]{1,0:T(8,128)} %bitcast.7, f32[1,1024]{1,0:T(1,128)} %bitcast.9, bf16[256,256]{1,0:T(8,128)(2,1)} %constant.4.clone.fwd, ...), custom_call_target="tpu_custom_call" | custom-call | tf_op jit(solution)/shard_map/hyena/pallas_call | solution.py:608
  68.7 1.7 %copy.10 = bf16[1024,128]{1,0:T(8,128)(2,1)} copy(bf16[1024,128]{1,0:T(8,128)(2,1)} %bitcast.5) | data formatting | bytes 524288

commit v4 on v3

--- a/solution.py
+++ b/solution.py
@@ -40,7 +40,7 @@
     proj_hbm, taps_hbm, amps_hbm, rates_hbm, skip, fwd, bwd, w_shard, out,
     proj, taps, amps, rates, ex, rev, first, ratio, wide, carry_w, rate_tiles,
     xs, halo_s, halo_r, prod, gate, local, s_send, s_recv, t_send, t_recv, starts, e_send, e_recv, p_send, p_recv,
-    gall, wg, acc, o_send, o_own,
+    gall, wg, acc, o_send,
     word_sem, in_sem, halo_sem, s_ssem, s_rsem, t_ssem, t_rsem, e_ssem, e_rsem, p_ssem, p_rsem,
     wx_sem, wf_rsem, wf_ssem, wb_rsem, wbz_ssem, wz_rsem, wz_ssem, wl_rsem, wr_rsem, wy_ssem, wh_rsem, wh_ssem, g_rsem, g_ssem, f_ssem, h_ssem, o_sem,
 ):
@@ -94,12 +94,14 @@
     down = at(xl, y, lax.rem(z + Z - ZL, Z))
     cx = at(xo, y, z)
 
+    for c in (up, down, nxt, prv, zr, zl):
+        hello(c, rep)
+
     @pl.loop(1, plane)
     def _(d):
         hello(plane_peer(lax.rem(mine + d, plane)), rep)
 
-    for c in (nxt, prv, zr, zl, up, down, cx):
-        hello(c, rep)
+    hello(cx, rep)
     hello(ctx, rep_core)
     hello(cx, rep_far)
     reads = [
@@ -224,6 +226,15 @@
             if k < RZ - 1 or p == 1:
                 b_round(p, k, 0, k).start()
 
+    def w_direct(d_z):
+        for i in range(2):
+            ssem = wh_ssem.at[i * Z + z_of(d_z)]
+            w_half(0, d_z, i, ssem, wh_rsem, at(xl, y_of(2), z)).start()
+
+    def w_sides(d_z):
+        w_whole(Y - 1, d_z, wx_sem.at[0], wl_rsem, ctx).wait_recv()
+        w_whole(1, d_z, wx_sem.at[0], wr_rsem, ctx).wait_recv()
+
     def w_start():
         own.wait()
         x_copy.wait_recv()
@@ -244,9 +255,9 @@
             w_arrived(k, i)
             if k < RZ - 1 or i == 1:
                 w_round(k, i, 0, k).start()
+        b_step(k - 1)
         w_spread(-k)
         w_spread(k)
-        b_step(k - 1)
         if k > 1:
             w_relay(2 - k)
         if k > 2:
@@ -255,6 +266,7 @@
     def w_last():
         for i in range(2):
             w_arrived(RZ, i)
+        w_direct(RZ)
         w_spread(RZ)
         b_step(RZ - 1)
         for k in (RZ - 2, RZ - 1):
@@ -394,8 +406,7 @@
     e_send[...] = share
     pl.semaphore_wait(word_sem.at[1], 2)
 
-    @pl.loop(1, ZH)
-    def _(d):
+    for d in (2, 1, 3):
         to = lax.rem(zh + d, ZH)
         remote(t_send, t_recv.at[zh], t_ssem.at[d], t_rsem.at[zh], slab_peer(xl, to)).start()
 
@@ -503,7 +514,7 @@
         g_pass(k)
     for p in range(2):
         b_arrived(p, RZ)
-    w_relay(RZ)
+    w_sides(RZ)
 
     @pl.loop(0, Z)
     def _(d):
@@ -547,9 +558,7 @@
     turn(xo, o_send)
     swap = remote(o_send, out.at[xl], o_sem.at[0], o_sem.at[1], cx)
     swap.start()
-    turn(xl, o_own)
-    keep_own = pltpu.make_async_copy(o_own, out.at[xl], o_sem.at[2])
-    keep_own.start()
+    turn(xl, out.at[xl])
 
     halo.wait_send()
     x_copy.wait_send()
@@ -591,7 +600,6 @@
     def _(i):
         g_copy(0, 0, 0, h_ssem.at[i], ctx, rep).wait_send()
 
-    keep_own.wait()
     swap.wait_send()
     remote(o_send, out.at[xo], o_sem.at[0], o_sem.at[1], ctx).wait_recv()
 
@@ -607,11 +615,11 @@
     dma = pltpu.SemaphoreType.DMA
     out = pl.pallas_call(
         kernel,
-        out_shape=jax.ShapeDtypeStruct((X, half, length), BF16),
+        out_shape=pltpu.VMEM((X, half, length), BF16),
         in_specs=[pl.BlockSpec(memory_space=pltpu.HBM)] * 4
         + [pl.BlockSpec(memory_space=vm)] * 3
         + [pl.BlockSpec(memory_space=pltpu.HBM)],
-        out_specs=pl.BlockSpec(memory_space=pl.ANY),
+        out_specs=pl.BlockSpec(memory_space=vm),
         scratch_shapes=[
             vm((3, chans, length), BF16),
             vm((3, 3, chans), F32),
@@ -643,7 +651,6 @@
             vm((X, Y, Z, rows, half), BF16),
             vm((X * length, half), F32),
             vm((half, length), BF16),
-            vm((half, length), BF16),
             pltpu.SemaphoreType.REGULAR((2,)),
             dma((6,)),
             dma((2,)),
@@ -671,7 +678,7 @@
             dma((3 * pieces,)),
             dma((3 * pieces,)),
             dma((pieces,)),
-            dma((3,)),
+            dma((2,)),
         ],
         compiler_params=pltpu.CompilerParams(
             collective_id=0, has_side_effects=True, vmem_limit_bytes=60 * 1024 * 1024

time: 70.6 us -> 68 us (0.963)
  Pallas kernels: 68.7 us -> 67.1 us
  local copies, waits for them, and re-layouts: 1.67 us -> 0.71 us
    pallas_call x1, Pallas kernels: 68.7 us -> 67.1 us  [per_device(): pl.pallas_call(kernel, out_shape=pltpu.VMEM((X, half, length), BF16), in_...]
    unnamed x1, local copies, waits for them, and re-layouts: 1.67 us -> 0.71 us
where the time goes in v4:
time: 68 us; the launch traced here: 67.8 us
  Pallas kernels  67.1 us (99%)
  local copies, waits for them, and re-layouts  0.71 us (1%)
    pallas_call x1, Pallas kernels, per_device(): pl.pallas_call(kernel, out_shape=pltpu.VMEM((X, half, length), BF16), in_...  67.1 us

profile of v4, /device:TPU:1, one launch (start us, length us, event | category | flops | bytes accessed | tf_op | source)
XLA Modules:
  0.0 67.8 jit_solution(10004577040093706014)
XLA Ops:
  0.0 67.1 %hyena.1 = bf16[2,512,128]{2,1,0:T(8,128)(2,1)S(1)} custom-call(bf16[3,1024,128]{2,1,0:T(8,128)(2,1)} %proj_hbm.1, f32[3,3,1024]{2,1,0:T(4,128)} %bitcast.8, f32[16,1024]{1,0:T(8,128)} %bitcast.6, f32[16,1024]{1,0:T(8,128)} %bitcast.7, f32[1,1024]{1,0:T(1,128)} %bitcast.9, bf16[256,256]{1,0:T(8,128)(2,1)} %constant.4.clone.fwd, ...), custom_call_target="tpu_custom_call" | custom-call | tf_op jit(solution)/shard_map/hyena/pallas_call | solution.py:616
  67.1 0.7 %copy.10 = bf16[1024,128]{1,0:T(8,128)(2,1)} copy(bf16[1024,128]{1,0:T(8,128)(2,1)S(1)} %bitcast.5) | data formatting | bytes 524288

commit v5 on v4

--- a/solution.py
+++ b/solution.py
@@ -12,7 +12,7 @@
 ZL = 4
 REPS = 4
 MODES = 16
-KC = 256
+KC = 512
 F32 = jnp.float32
 BF16 = jnp.bfloat16
 
@@ -520,9 +520,10 @@
     def _(d):
         w_relayed(d)
 
-    def project(r_, here):
+    def project(r_, here, cols=slice(None)):
         n = r_ * (chans // rows) // Z
-        part = wg[n // Y, pl.ds(lax.rem(n, Y), chans // rows // Z)].reshape(chans, half)
+        part = wg[n // Y, pl.ds(lax.rem(n, Y), chans // rows // Z), :, :, cols]
+        part = part.reshape(chans, part.shape[-1])
         return jnp.dot(gall[r_, here, :], part, preferred_element_type=F32)
 
     both = pl.ds(0, X * length)
@@ -548,17 +549,23 @@
         for x_ in range(X):
             g_arrived(x_, core_far, k)
 
-    def turn(x_, to):
+    def turn(x_, i, to):
         here = pl.ds(pl.multiple_of(x_ * length, length), length)
-        acc[here, :] += project(core_far, here)
-        for i in range(half // 128):
-            cols = pl.ds(128 * i, 128)
-            to[cols, :] = acc[here, cols].T.astype(BF16)
-
-    turn(xo, o_send)
-    swap = remote(o_send, out.at[xl], o_sem.at[0], o_sem.at[1], cx)
-    swap.start()
-    turn(xl, out.at[xl])
+        cols = pl.ds(i * (half // 2), half // 2)
+        done = acc[here, cols] + project(core_far, here, cols)
+        to[cols, :] = done.T.astype(BF16)
+
+    def swapped(i, x_, c):
+        cols = pl.ds(i * (half // 2), half // 2)
+        return remote(
+            o_send.at[cols, :], out.at[x_, cols, :], o_sem.at[i], o_sem.at[2 + i], c
+        )
+
+    for i in range(2):
+        turn(xo, i, o_send)
+        swapped(i, xl, cx).start()
+    for i in range(2):
+        turn(xl, i, out.at[xl])
 
     halo.wait_send()
     x_copy.wait_send()
@@ -600,8 +607,9 @@
     def _(i):
         g_copy(0, 0, 0, h_ssem.at[i], ctx, rep).wait_send()
 
-    swap.wait_send()
-    remote(o_send, out.at[xo], o_sem.at[0], o_sem.at[1], ctx).wait_recv()
+    for i in range(2):
+        swapped(i, xl, cx).wait_send()
+        swapped(i, xo, ctx).wait_recv()
 
 
 def per_device(projected, short_taps, residues, decay_rates, skip_gain, out_weight):
@@ -678,7 +686,7 @@
             dma((3 * pieces,)),
             dma((3 * pieces,)),
             dma((pieces,)),
-            dma((2,)),
+            dma((4,)),
         ],
         compiler_params=pltpu.CompilerParams(
             collective_id=0, has_side_effects=True, vmem_limit_bytes=60 * 1024 * 1024

time: 68 us -> 68.1 us (level)
  no operation moved by 1% of the time
where the time goes in v5:
time: 68.1 us; the launch traced here: 67.9 us
  Pallas kernels  67.2 us (99%)
  local copies, waits for them, and re-layouts  0.71 us (1%)
    pallas_call x1, Pallas kernels, per_device(): pl.pallas_call(kernel, out_shape=pltpu.VMEM((X, half, length), BF16), in_...  67.2 us

profile of v5, /device:TPU:1, one launch (start us, length us, event | category | flops | bytes accessed | tf_op | source)
XLA Modules:
  0.0 67.9 jit_solution(3995613438352858070)
XLA Ops:
  0.0 67.2 %hyena.1 = bf16[2,512,128]{2,1,0:T(8,128)(2,1)S(1)} custom-call(bf16[3,1024,128]{2,1,0:T(8,128)(2,1)} %proj_hbm.1, f32[3,3,1024]{2,1,0:T(4,128)} %bitcast.8, f32[16,1024]{1,0:T(8,128)} %bitcast.6, f32[16,1024]{1,0:T(8,128)} %bitcast.7, f32[1,1024]{1,0:T(1,128)} %bitcast.9, bf16[256,256]{1,0:T(8,128)(2,1)} %constant.4.clone.fwd, ...), custom_call_target="tpu_custom_call" | custom-call | tf_op jit(solution)/shard_map/hyena/pallas_call | solution.py:624
  67.2 0.7 %copy.10 = bf16[1024,128]{1,0:T(8,128)(2,1)} copy(bf16[1024,128]{1,0:T(8,128)(2,1)S(1)} %bitcast.5) | data formatting | bytes 524288
